TPU v7x, 256 devices: a whole 4x4x8 slice. The times are simulated.
256 devices in a mesh: branch: 2 (over z_lo), seq: 128 (over y, x, z_hi, core).
Axes of the slice: x: 4, y: 4, z: 8 (z_hi: 4, z_lo: 2; z = z_hi * 2 + z_lo), core: 2. Of those that a mesh axis runs over, the one named last changes fastest.
Arguments:
- queries: bfloat16 [4, 2048, 5120], P('branch', 'seq'), may hold values from -40 to 40
- keys: bfloat16 [4, 2048, 5120], P('branch', 'seq'), may hold values from -8 to 8
- values: bfloat16 [4, 2048, 5120], P('branch', 'seq'), may hold values from -6 to 6
- output_weight_matrix: bfloat16 [5120, 5120], P('seq'), may hold values from -0.078125 to 0.078125
- style_down_maps: bfloat16 [4, 5120, 64], P(None, 'seq'), may hold values from -0.078125 to 0.078125
- style_up_maps: bfloat16 [4, 64, 5120], replicated, may hold values from -0.75 to 0.75
- branch_adapter: int32 [4], replicated, may hold values from 0 to 3
- guidance_weight_eighths: int32 [4], replicated, may hold values from -8 to 24
- gate_offset_learned: float32 [5120], P('branch'), may hold values from -3 to 3
- timestep: int32 [1], replicated, may hold values from 0 to 999
Outputs:
- guided: bfloat16 [2048, 5120], P('seq', 'branch')
All inputs are finite; a program needn't handle non-finite values.
Results may differ from a plain program's by a relative error of at most 0.019.
Values may be sent and summed in bfloat16 or wider, within the bound.
A program may use at most 128 MiB of HBM per device.

v0:
```python
import math

import jax
import jax.numpy as jnp
from jax import lax
from jax.sharding import PartitionSpec as P

HEAD_DIM = 128
UDEG = 8


guide_unit = 0.125


def passed_along(x, axis, by):
    count = lax.axis_size(axis)
    return lax.ppermute(x, axis, [(i, (i + by) % count) for i in range(count)])


def from_partner(value, axis, bit):
    mask = 2**bit
    pairs = [(source, source ^ mask) for source in range(lax.axis_size(axis))]
    return lax.ppermute(value, axis, pairs)


def fold_keys(state_now, query_rows, key_piece, value_piece, score_scale):
    running_max, running_sum, summed = state_now
    scores = (
        jnp.einsum("bhqd,bhkd->bhqk", query_rows, key_piece, preferred_element_type=jnp.float32)
        * score_scale
    )
    new_max = jnp.maximum(running_max, jnp.max(scores, axis=3))
    factor = jnp.exp(running_max - new_max)
    weights = jnp.exp(scores - new_max[..., None])
    running_sum = running_sum * factor + jnp.sum(weights, axis=3)
    summed = summed * factor[..., None] + jnp.einsum(
        "bhqk,bhkd->bhqd",
        weights.astype(jnp.bfloat16),
        value_piece,
        preferred_element_type=jnp.float32,
    )
    return (new_max, running_sum, summed)


def join_rows(held, got, upper_half, axis_index):
    return jnp.where(
        upper_half,
        jnp.concatenate([got, held], axis=axis_index),
        jnp.concatenate([held, got], axis=axis_index),
    )


def shards(
    queries,
    keys,
    values,
    output_weight_matrix,
    style_down_maps,
    style_up_maps,
    branch_adapter,
    guidance_weight_eighths,
    gate_offset_learned,
    timestep,
):
    seq_count = lax.axis_size("seq")
    rotation_length = seq_count // UDEG
    cycle_bits = rotation_length.bit_length() - 1
    position = lax.axis_index("seq")
    group_pos = position // rotation_length
    cycle_pos = position % rotation_length
    branch_pos = lax.axis_index("branch")
    local_branches, tok_count, width = queries.shape
    group_width = width // UDEG
    head_count = group_width // HEAD_DIM
    rows_here = UDEG * tok_count
    stacked = jnp.stack([queries, keys, values])
    arrived = []
    for offset in range(UDEG):
        target = (group_pos + offset) % UDEG
        block_piece = lax.dynamic_slice_in_dim(stacked, target * group_width, group_width, 3)
        if offset == 0:
            arrived.append(block_piece)
        else:
            arrived.append(passed_along(block_piece, "seq", rotation_length * offset))
    sources = (group_pos - jnp.arange(UDEG, dtype=jnp.int32)) % UDEG
    by_source = jnp.take(jnp.stack(arrived), sources, axis=0)

    def to_heads(block_set):
        return (
            block_set.reshape(UDEG, local_branches, tok_count, head_count, HEAD_DIM)
            .transpose(1, 3, 0, 2, 4)
            .reshape(local_branches, head_count, rows_here, HEAD_DIM)
        )

    query_rows = to_heads(by_source[:, 0])
    key_rows = to_heads(by_source[:, 1])
    value_rows = to_heads(by_source[:, 2])
    score_scale = HEAD_DIM ** (-0.5)
    state_now = (
        jnp.full((local_branches, head_count, rows_here), -jnp.inf, jnp.float32),
        jnp.zeros((local_branches, head_count, rows_here), jnp.float32),
        jnp.zeros((local_branches, head_count, rows_here, HEAD_DIM), jnp.float32),
    )
    state_now = fold_keys(state_now, query_rows, key_rows, value_rows, score_scale)
    rows_per_worker = output_weight_matrix.shape[0]
    bit_order = list(range(cycle_bits))
    key_held, value_held = (key_rows, value_rows)
    weight_held = output_weight_matrix[None]
    down_matrix_kept = style_down_maps[None]
    for step_index in range(cycle_bits):
        bit_index = bit_order[step_index]
        upper_half = cycle_pos // 2**bit_index % 2 == 1
        key_got, value_got, weight_got, down_got = from_partner(
            (key_held, value_held, weight_held, down_matrix_kept), "seq", bit_index
        )
        state_now = fold_keys(state_now, query_rows, key_got, value_got, score_scale)
        if step_index + 1 < cycle_bits:
            key_held = jnp.concatenate([key_held, key_got], axis=2)
            value_held = jnp.concatenate([value_held, value_got], axis=2)
        weight_held = join_rows(weight_held, weight_got, upper_half, 0)
        down_matrix_kept = join_rows(down_matrix_kept, down_got, upper_half, 0)
    group_weight = weight_held.reshape(rotation_length * rows_per_worker, width)
    group_down = down_matrix_kept.transpose(1, 0, 2, 3).reshape(
        style_down_maps.shape[0], rotation_length * rows_per_worker, style_down_maps.shape[2]
    )
    running_max, running_sum, summed = state_now
    attended = (summed / running_sum[..., None]).astype(jnp.bfloat16)
    attended = attended.transpose(0, 2, 1, 3).reshape(local_branches, rows_here, group_width)
    adapter_total = style_up_maps.shape[0]
    local_ids = lax.dynamic_slice_in_dim(
        branch_adapter, branch_pos * local_branches, local_branches, 0
    )
    adapter_chooser = (
        local_ids[:, None] == jnp.arange(adapter_total, dtype=jnp.int32)[None, :]
    ).astype(jnp.bfloat16)
    chosen_down_map = jnp.einsum(
        "bn,ncr->bcr", adapter_chooser, group_down, preferred_element_type=jnp.float32
    ).astype(jnp.bfloat16)
    chosen_up_map = jnp.einsum(
        "hm,mig->hig", adapter_chooser, style_up_maps, preferred_element_type=jnp.float32
    ).astype(jnp.bfloat16)
    plain_output = jnp.dot(
        attended.reshape(local_branches * rows_here, group_width),
        group_weight,
        preferred_element_type=jnp.float32,
    ).reshape(local_branches, rows_here, width)
    reduced_features = jnp.einsum(
        "bqc,bcr->bqr", attended, chosen_down_map, preferred_element_type=jnp.float32
    ).astype(jnp.bfloat16)
    partial_out = (
        plain_output
        + jnp.einsum(
            "xim,xmo->xio", reduced_features, chosen_up_map, preferred_element_type=jnp.float32
        )
    ).astype(jnp.bfloat16)
    partial_out = partial_out.reshape(local_branches, UDEG, tok_count, width)
    combined = jnp.zeros((local_branches, tok_count, width), jnp.float32)
    for offset in range(UDEG):
        target = (group_pos + offset) % UDEG
        block_piece = lax.dynamic_index_in_dim(partial_out, target, 1, keepdims=False)
        if offset == 0:
            combined = block_piece.astype(jnp.float32)
        else:
            combined = combined + passed_along(block_piece, "seq", rotation_length * offset).astype(
                jnp.float32
            )
    local_weights = (
        lax.dynamic_slice_in_dim(
            guidance_weight_eighths, branch_pos * local_branches, local_branches, 0
        ).astype(jnp.float32)
        * guide_unit
    )
    mixture = jnp.einsum("b,btd->td", local_weights, combined)
    halves = lax.psum_scatter(
        mixture.astype(jnp.bfloat16), "branch", scatter_dimension=1, tiled=True
    ).astype(jnp.float32)
    column_count = halves.shape[1]
    columns = branch_pos * column_count + jnp.arange(column_count, dtype=jnp.int32)
    half_width = width // 2
    frequency = jnp.exp(
        (columns % half_width).astype(jnp.float32) * (-math.log(10000.0) / half_width)
    )
    angles = timestep.astype(jnp.float32)[0] * frequency
    gate_row = gate_offset_learned + jnp.where(
        columns < half_width, jnp.cos(angles), jnp.sin(angles)
    )
    return (halves * gate_row[None, :]).astype(jnp.bfloat16)


def solution(mesh):
    placed = (
        P("branch", "seq", None),
        P("branch", "seq", None),
        P("branch", "seq", None),
        P("seq", None),
        P(None, "seq", None),
        P(),
        P(),
        P(),
        P("branch"),
        P(),
    )
    return jax.shard_map(
        shards, mesh=mesh, in_specs=placed, out_specs=P("seq", "branch"), check_vma=False
    )
```

profile of v0, /device:TPU:1, one launch (start us, length us, event | category | flops | bytes accessed | tf_op | source)
XLA Modules:
  0.0 501.9 jit_solution(11476579859901169176)
XLA Ops:
  6.5 2.4 pad_maximum_fusion.4
  8.9 2.1 constant_dynamic-slice_fusion
  11.0 3.6 collective-permute-start
  15.9 2.0 collective-permute-start.2
  17.9 1.6 collective-permute-start.3
  19.4 4.5 collective-permute-start.4
  24.0 1.6 bitcast_dynamic-update-slice_fusion.7
  33.1 2.8 gather_fusion
  38.8 3.6 collective-permute-start.7
  44.6 3.0 collective-permute-start.9
  48.2 2.2 reshape_squeeze.11
  50.4 1.8 copy.19
  52.2 1.9 copy.22
  55.7 24.5 %collective-permute-done.20 = bf16[2,4,40,64]{3,2,1,0:T(8,128)(2,1)} collective-permute-done((bf16[2,4,40,64]{3,2,1,0:T(8,128)(2,1)S(1)}, bf16[2,4,40,64]{3,2,1,0:T(8,128)(2,1)}, u32[]{:S(2)}, u32[]{:S(2)}) %collective-permute-start.20) | collective-permute-done | bytes 40992 | tf_op jit(solution)/shard_map/ppermute | solution.py:23
  81.2 6.3 %collective-permute-start.21 = (bf16[4,4,40,64]{3,2,1,0:T(8,128)(2,1)S(1)}, bf16[4,4,40,64]{3,2,1,0:T(8,128)(2,1)}, u32[]{:S(2)}, u32[]{:S(2)}) collective-permute-start(bf16[4,4,40,64]{3,2,1,0:T(8,128)(2,1)S(1)} %maximum_select_fusion.6), channel_id=1, source_target_pairs={{0,4},{1,5},{2,6},{3,7},{4,0},{5,1},{6,2},{7,3},{8,12},{9,13},{10,... | collective-permute-start | bytes 245768 | tf_op jit(solution)/shard_map/ppermute | solution.py:23
  87.6 2.3 pad_maximum_fusion.2
  90.1 1.9 pad_maximum_fusion.6
  92.0 2.2 maximum_select_fusion.3
  94.2 2.4 collective-permute-start.16
  96.6 4.5 fusion.7
  104.2 93.1 %collective-permute-done.10 = bf16[2,5,256,128]{2,3,1,0:T(8,128)(2,1)} collective-permute-done((bf16[2,5,256,128]{2,3,1,0:T(8,128)(2,1)}, bf16[2,5,256,128]{2,3,1,0:T(8,128)(2,1)}, u32[]{:S(2)}, u32[]{:S(2)}) %collective-permute-start.10) | collective-permute-done | bytes 655392 | tf_op jit(solution)/shard_map/ppermute | solution.py:23
  197.3 2.4 pad_maximum_fusion.3
  199.7 3.2 collective-permute-start.12
  202.9 2.8 pad_maximum_fusion
  206.0 37.4 %collective-permute-done.16 = bf16[2,40,5120]{2,1,0:T(8,128)(2,1)} collective-permute-done((bf16[2,40,5120]{2,1,0:T(8,128)(2,1)}, bf16[2,40,5120]{2,1,0:T(8,128)(2,1)}, u32[]{:S(2)}, u32[]{:S(2)}) %collective-permute-start.16) | collective-permute-done | bytes 819232 | tf_op jit(solution)/shard_map/ppermute | solution.py:23
  243.4 2.2 maximum_select_fusion.2
  245.6 3.3 collective-permute-start.17
  250.6 2.1 copy.33
  256.9 1.7 pad_maximum_fusion.1
  259.0 2.0 multiply_reduce_fusion.1
  261.0 82.8 %collective-permute-done.17 = bf16[4,40,5120]{2,1,0:T(8,128)(2,1)} collective-permute-done((bf16[4,40,5120]{2,1,0:T(8,128)(2,1)S(1)}, bf16[4,40,5120]{2,1,0:T(8,128)(2,1)}, u32[]{:S(2)}, u32[]{:S(2)}) %collective-permute-start.17) | collective-permute-done | bytes 1638432 | tf_op jit(solution)/shard_map/ppermute | solution.py:23
  343.8 2.4 maximum_select_fusion.1
  346.2 9.2 %collective-permute-start.18 = (bf16[8,40,5120]{2,1,0:T(8,128)(2,1)S(1)}, bf16[8,40,5120]{2,1,0:T(8,128)(2,1)}, u32[]{:S(2)}, u32[]{:S(2)}) collective-permute-start(bf16[8,40,5120]{2,1,0:T(8,128)(2,1)S(1)} %maximum_select_fusion.1), channel_id=1, source_target_pairs={{0,8},{1,9},{2,10},{3,11},{4,12},{5,13},{6,14},{7,15},{8,0},{9,1},... | collective-permute-start | bytes 9830408 | tf_op jit(solution)/shard_map/ppermute | solution.py:23
  355.4 2.7 multiply_reduce_fusion
  362.4 2.0 fusion.29
  365.8 2.1 fusion.32
  367.9 5.0 fusion.13
  372.8 54.4 %collective-permute-done.18 = bf16[8,40,5120]{2,1,0:T(8,128)(2,1)} collective-permute-done((bf16[8,40,5120]{2,1,0:T(8,128)(2,1)S(1)}, bf16[8,40,5120]{2,1,0:T(8,128)(2,1)}, u32[]{:S(2)}, u32[]{:S(2)}) %collective-permute-start.18) | collective-permute-done | bytes 3276832 | tf_op jit(solution)/shard_map/ppermute | solution.py:23
  427.2 4.2 maximum_select_fusion
  431.7 4.0 fusion
  435.7 2.6 dynamic-slice_bitcast_fusion.6
  438.3 2.7 collective-permute-start.29
  441.0 2.2 collective-permute-start.27
  445.1 2.5 collective-permute-done.29
  450.1 15.3 %collective-permute-start.23 = (bf16[2,16,5120]{2,1,0:T(8,128)(2,1)S(1)}, bf16[2,16,5120]{2,1,0:T(8,128)(2,1)}, u32[]{:S(2)}, u32[]{:S(2)}) collective-permute-start(bf16[2,16,5120]{2,1,0:T(8,128)(2,1)S(1)} %get-tuple-element.14), channel_id=1, source_target_pairs={{0,16},{1,17},{2,18},{3,19},{4,20},{5,21},{6,22},{7,23},{8,24},{9,... | collective-permute-start | bytes 983048 | tf_op jit(solution)/shard_map/ppermute | solution.py:17
  465.4 5.0 %collective-permute-done.24 = bf16[2,16,5120]{2,1,0:T(8,128)(2,1)} collective-permute-done((bf16[2,16,5120]{2,1,0:T(8,128)(2,1)S(1)}, bf16[2,16,5120]{2,1,0:T(8,128)(2,1)}, u32[]{:S(2)}, u32[]{:S(2)}) %collective-permute-start.24) | collective-permute-done | bytes 327712 | tf_op jit(solution)/shard_map/ppermute | solution.py:17
  470.5 2.0 fusion.42
  474.6 18.7 %reduce-scatter.2.cloned.1.call-done = bf16[16,2560]{1,0:T(8,128)(2,1)} async-done(((bf16[16,5120]{1,0:T(8,128)(2,1)}), bf16[16,2560]{1,0:T(8,128)(2,1)}) %reduce-scatter.2.cloned.1.call-update) | async-done | bytes 81936 | tf_op jit(solution)/shard_map/reduce_scatter | solution.py:174
  (125 shorter events, 40.3 us)
Async XLA Ops:
  6.5 90.0 %copy-start = (bf16[4,64,5120]{2,1,0:T(8,128)(2,1)S(1)}, bf16[4,64,5120]{2,1,0:T(8,128)(2,1)}, u32[]{:S(2)}) copy-start(bf16[4,64,5120]{2,1,0:T(8,128)(2,1)} %param.15) | copy-start | bytes 7864324
  6.5 486.7 %reduce-scatter.2.cloned.1.call-start = ((), (), s32[]{:S(2)}) async-start(), calls=%async_computation.1 | async-start | bytes 245760 | tf_op jit(solution)/shard_map/reduce_scatter | solution.py:174
  11.0 14.5 %collective-permute-start = (bf16[3,2,16,640]{3,2,1,0:T(8,128)(2,1)}, bf16[3,2,16,640]{3,2,1,0:T(8,128)(2,1)S(1)}, u32[]{:S(2)}, u32[]{:S(2)}) collective-permute-start(bf16[3,2,16,640]{3,2,1,0:T(8,128)(2,1)} %get-tuple-element.30), channel_id=1, source_target_pairs={{0,16},{1,17},{2,18},{3,19},{4,20},{5,21},{6,22},{7,23},{8,24},{9,... | collective-permute-start | bytes 368648 | tf_op jit(solution)/shard_map/ppermute | solution.py:17
  14.6 12.6 %collective-permute-start.1 = (bf16[3,2,16,640]{3,2,1,0:T(8,128)(2,1)}, bf16[3,2,16,640]{3,2,1,0:T(8,128)(2,1)S(1)}, u32[]{:S(2)}, u32[]{:S(2)}) collective-permute-start(bf16[3,2,16,640]{3,2,1,0:T(8,128)(2,1)} %get-tuple-element.29), channel_id=1, source_target_pairs={{0,32},{1,33},{2,34},{3,35},{4,36},{5,37},{6,38},{7,39},{8,40},{9,... | collective-permute-start | bytes 368648 | tf_op jit(solution)/shard_map/ppermute | solution.py:17
  15.9 12.0 %collective-permute-start.2 = (bf16[3,2,16,640]{3,2,1,0:T(8,128)(2,1)}, bf16[3,2,16,640]{3,2,1,0:T(8,128)(2,1)S(1)}, u32[]{:S(2)}, u32[]{:S(2)}) collective-permute-start(bf16[3,2,16,640]{3,2,1,0:T(8,128)(2,1)} %get-tuple-element.28), channel_id=1, source_target_pairs={{0,48},{1,49},{2,50},{3,51},{4,52},{5,53},{6,54},{7,55},{8,56},{9,... | collective-permute-start | bytes 368648 | tf_op jit(solution)/shard_map/ppermute | solution.py:17
  17.9 12.2 %collective-permute-start.3 = (bf16[3,2,16,640]{3,2,1,0:T(8,128)(2,1)}, bf16[3,2,16,640]{3,2,1,0:T(8,128)(2,1)S(1)}, u32[]{:S(2)}, u32[]{:S(2)}) collective-permute-start(bf16[3,2,16,640]{3,2,1,0:T(8,128)(2,1)} %get-tuple-element.27), channel_id=1, source_target_pairs={{0,64},{1,65},{2,66},{3,67},{4,68},{5,69},{6,70},{7,71},{8,72},{9,... | collective-permute-start | bytes 368648 | tf_op jit(solution)/shard_map/ppermute | solution.py:17
  19.4 11.3 %collective-permute-start.4 = (bf16[3,2,16,640]{3,2,1,0:T(8,128)(2,1)}, bf16[3,2,16,640]{3,2,1,0:T(8,128)(2,1)S(1)}, u32[]{:S(2)}, u32[]{:S(2)}) collective-permute-start(bf16[3,2,16,640]{3,2,1,0:T(8,128)(2,1)} %get-tuple-element.26), channel_id=1, source_target_pairs={{0,80},{1,81},{2,82},{3,83},{4,84},{5,85},{6,86},{7,87},{8,88},{9,... | collective-permute-start | bytes 368648 | tf_op jit(solution)/shard_map/ppermute | solution.py:17
  25.5 6.1 %collective-permute-start.5 = (bf16[3,2,16,640]{3,2,1,0:T(8,128)(2,1)S(1)}, bf16[3,2,16,640]{3,2,1,0:T(8,128)(2,1)S(1)}, u32[]{:S(2)}, u32[]{:S(2)}) collective-permute-start(bf16[3,2,16,640]{3,2,1,0:T(8,128)(2,1)S(1)} %get-tuple-element.25), channel_id=1, source_target_pairs={{0,96},{1,97},{2,98},{3,99},{4,100},{5,101},{6,102},{7,103},{8,104... | collective-permute-start | bytes 368648 | tf_op jit(solution)/shard_map/ppermute | solution.py:17
  27.3 5.2 %collective-permute-start.6 = (bf16[3,2,16,640]{3,2,1,0:T(8,128)(2,1)S(1)}, bf16[3,2,16,640]{3,2,1,0:T(8,128)(2,1)S(1)}, u32[]{:S(2)}, u32[]{:S(2)}) collective-permute-start(bf16[3,2,16,640]{3,2,1,0:T(8,128)(2,1)S(1)} %get-tuple-element.24), channel_id=1, source_target_pairs={{0,112},{1,113},{2,114},{3,115},{4,116},{5,117},{6,118},{7,119},{8... | collective-permute-start | bytes 368648 | tf_op jit(solution)/shard_map/ppermute | solution.py:17
  37.4 10.2 %copy-start.17 = (bf16[4,40,64]{2,1,0:T(8,128)(2,1)S(1)}, bf16[4,40,64]{2,1,0:T(8,128)(2,1)}, u32[]{:S(2)}) copy-start(bf16[4,40,64]{2,1,0:T(8,128)(2,1)} %param.14) | copy-start | bytes 61444
  38.4 17.2 %copy-start.19 = (s32[4]{0:T(128)S(1)}, s32[4]{0:T(128)}, u32[]{:S(2)}) copy-start(s32[4]{0:T(128)} %param.16) | copy-start | bytes 52
  38.8 4.8 collective-permute-start.7
  44.6 43.0 %collective-permute-start.9 = (bf16[2,5,256,128]{3,2,1,0:T(8,128)(2,1)}, bf16[2,5,256,128]{3,2,1,0:T(8,128)(2,1)}, u32[]{:S(2)}, u32[]{:S(2)}) collective-permute-start(bf16[2,5,256,128]{3,2,1,0:T(8,128)(2,1)} %pad_maximum_fusion.5), channel_id=1, source_target_pairs={{0,2},{1,3},{2,0},{3,1},{4,6},{5,7},{6,4},{7,5},{8,10},{9,11},{10,... | collective-permute-start | bytes 1966088 | tf_op jit(solution)/shard_map/ppermute | solution.py:23
  47.6 6.5 %collective-permute-start.19 = (bf16[1,4,40,64]{3,2,1,0:T(8,128)(2,1)S(1)}, bf16[1,4,40,64]{3,2,1,0:T(8,128)(2,1)S(1)}, u32[]{:S(2)}, u32[]{:S(2)}) collective-permute-start(bf16[1,4,40,64]{3,2,1,0:T(8,128)(2,1)S(1)} %bitcast.244), channel_id=1, source_target_pairs={{0,1},{1,0},{2,3},{3,2},{4,5},{5,4},{6,7},{7,6},{8,9},{9,8},{10,11... | collective-permute-start | bytes 61448 | tf_op jit(solution)/shard_map/ppermute | solution.py:23
  54.0 36.1 %collective-permute-start.8 = (bf16[2,5,128,128]{2,3,1,0:T(8,128)(2,1)}, bf16[2,5,128,128]{2,3,1,0:T(8,128)(2,1)}, u32[]{:S(2)}, u32[]{:S(2)}) collective-permute-start(bf16[2,5,128,128]{2,3,1,0:T(8,128)(2,1)} %copy.22), channel_id=1, source_target_pairs={{0,1},{1,0},{2,3},{3,2},{4,5},{5,4},{6,7},{7,6},{8,9},{9,8},{10,11... | collective-permute-start | bytes 983048 | tf_op jit(solution)/shard_map/ppermute | solution.py:23
  54.9 25.3 %collective-permute-start.20 = (bf16[2,4,40,64]{3,2,1,0:T(8,128)(2,1)S(1)}, bf16[2,4,40,64]{3,2,1,0:T(8,128)(2,1)}, u32[]{:S(2)}, u32[]{:S(2)}) collective-permute-start(bf16[2,4,40,64]{3,2,1,0:T(8,128)(2,1)S(1)} %maximum_select_fusion.7), channel_id=1, source_target_pairs={{0,2},{1,3},{2,0},{3,1},{4,6},{5,7},{6,4},{7,5},{8,10},{9,11},{10,... | collective-permute-start | bytes 122888 | tf_op jit(solution)/shard_map/ppermute | solution.py:23
  55.0 37.0 %collective-permute-start.15 = (bf16[1,40,5120]{2,1,0:T(8,128)(2,1)}, bf16[1,40,5120]{2,1,0:T(8,128)(2,1)}, u32[]{:S(2)}, u32[]{:S(2)}) collective-permute-start(bf16[1,40,5120]{2,1,0:T(8,128)(2,1)} %bitcast.238), channel_id=1, source_target_pairs={{0,1},{1,0},{2,3},{3,2},{4,5},{5,4},{6,7},{7,6},{8,9},{9,8},{10,11... | collective-permute-start | bytes 1228808 | tf_op jit(solution)/shard_map/ppermute | solution.py:23
  55.6 34.5 %copy-start.9 = (bf16[2,5,128,128]{2,3,1,0:T(8,128)(2,1)S(1)}, bf16[2,5,128,128]{2,3,1,0:T(8,128)(2,1)}, u32[]{:S(2)}) copy-start(bf16[2,5,128,128]{2,3,1,0:T(8,128)(2,1)} %copy.22) | copy-start | bytes 983044
  55.6 36.4 %copy-start.14 = (bf16[40,5120]{1,0:T(8,128)(2,1)S(1)}, bf16[40,5120]{1,0:T(8,128)(2,1)}, u32[]{:S(2)}) copy-start(bf16[40,5120]{1,0:T(8,128)(2,1)} %param.13) | copy-start | bytes 1228804
  81.2 21.3 %collective-permute-start.21 = (bf16[4,4,40,64]{3,2,1,0:T(8,128)(2,1)S(1)}, bf16[4,4,40,64]{3,2,1,0:T(8,128)(2,1)}, u32[]{:S(2)}, u32[]{:S(2)}) collective-permute-start(bf16[4,4,40,64]{3,2,1,0:T(8,128)(2,1)S(1)} %maximum_select_fusion.6), channel_id=1, source_target_pairs={{0,4},{1,5},{2,6},{3,7},{4,0},{5,1},{6,2},{7,3},{8,12},{9,13},{10,... | collective-permute-start | bytes 245768 | tf_op jit(solution)/shard_map/ppermute | solution.py:23
  89.9 113.1 %collective-permute-start.11 = (bf16[2,5,512,128]{3,2,1,0:T(8,128)(2,1)}, bf16[2,5,512,128]{3,2,1,0:T(8,128)(2,1)}, u32[]{:S(2)}, u32[]{:S(2)}) collective-permute-start(bf16[2,5,512,128]{3,2,1,0:T(8,128)(2,1)} %pad_maximum_fusion.2), channel_id=1, source_target_pairs={{0,4},{1,5},{2,6},{3,7},{4,0},{5,1},{6,2},{7,3},{8,12},{9,13},{10,... | collective-permute-start | bytes 3932168 | tf_op jit(solution)/shard_map/ppermute | solution.py:23
  92.0 105.3 %collective-permute-start.10 = (bf16[2,5,256,128]{2,3,1,0:T(8,128)(2,1)}, bf16[2,5,256,128]{2,3,1,0:T(8,128)(2,1)}, u32[]{:S(2)}, u32[]{:S(2)}) collective-permute-start(bf16[2,5,256,128]{2,3,1,0:T(8,128)(2,1)} %pad_maximum_fusion.6), channel_id=1, source_target_pairs={{0,2},{1,3},{2,0},{3,1},{4,6},{5,7},{6,4},{7,5},{8,10},{9,11},{10,... | collective-permute-start | bytes 1966088 | tf_op jit(solution)/shard_map/ppermute | solution.py:23
  94.2 149.2 %collective-permute-start.16 = (bf16[2,40,5120]{2,1,0:T(8,128)(2,1)}, bf16[2,40,5120]{2,1,0:T(8,128)(2,1)}, u32[]{:S(2)}, u32[]{:S(2)}) collective-permute-start(bf16[2,40,5120]{2,1,0:T(8,128)(2,1)} %maximum_select_fusion.3), channel_id=1, source_target_pairs={{0,2},{1,3},{2,0},{3,1},{4,6},{5,7},{6,4},{7,5},{8,10},{9,11},{10,... | collective-permute-start | bytes 2457608 | tf_op jit(solution)/shard_map/ppermute | solution.py:23
  101.0 96.3 %copy-start.10 = (bf16[2,5,128,128]{2,3,1,0:T(8,128)(2,1)S(1)}, bf16[2,5,128,128]{2,3,1,0:T(8,128)(2,1)}, u32[]{:S(2)}) copy-start(bf16[2,5,128,128]{2,3,1,0:T(8,128)(2,1)} %copy.22) | copy-start | bytes 983044
  102.5 156.6 %copy-start.3 = (bf16[2,5,8,16,128]{4,3,2,1,0:T(8,128)(2,1)}, bf16[2,5,8,16,128]{4,3,2,1,0:T(8,128)(2,1)S(1)}, u32[]{:S(2)}) copy-start(bf16[2,5,8,16,128]{4,3,2,1,0:T(8,128)(2,1)S(1)} %copy.17) | copy-start | bytes 983044
  103.8 145.6 %collective-permute-start.22 = (bf16[8,4,40,64]{3,2,1,0:T(8,128)(2,1)S(1)}, bf16[8,4,40,64]{3,2,1,0:T(8,128)(2,1)S(1)}, u32[]{:S(2)}, u32[]{:S(2)}) collective-permute-start(bf16[8,4,40,64]{3,2,1,0:T(8,128)(2,1)S(1)} %maximum_select_fusion.5), channel_id=1, source_target_pairs={{0,8},{1,9},{2,10},{3,11},{4,12},{5,13},{6,14},{7,15},{8,0},{9,1},... | collective-permute-start | bytes 491528 | tf_op jit(solution)/shard_map/ppermute | solution.py:23
  199.7 57.2 %collective-permute-start.12 = (bf16[2,5,512,128]{2,3,1,0:T(8,128)(2,1)}, bf16[2,5,512,128]{2,3,1,0:T(8,128)(2,1)}, u32[]{:S(2)}, u32[]{:S(2)}) collective-permute-start(bf16[2,5,512,128]{2,3,1,0:T(8,128)(2,1)} %pad_maximum_fusion.3), channel_id=1, source_target_pairs={{0,4},{1,5},{2,6},{3,7},{4,0},{5,1},{6,2},{7,3},{8,12},{9,13},{10,... | collective-permute-start | bytes 3932168 | tf_op jit(solution)/shard_map/ppermute | solution.py:23
  205.7 149.7 %collective-permute-start.13 = (bf16[2,5,1024,128]{3,2,1,0:T(8,128)(2,1)}, bf16[2,5,1024,128]{3,2,1,0:T(8,128)(2,1)}, u32[]{:S(2)}, u32[]{:S(2)}) collective-permute-start(bf16[2,5,1024,128]{3,2,1,0:T(8,128)(2,1)} %pad_maximum_fusion), channel_id=1, source_target_pairs={{0,8},{1,9},{2,10},{3,11},{4,12},{5,13},{6,14},{7,15},{8,0},{9,1},... | collective-permute-start | bytes 7864328 | tf_op jit(solution)/shard_map/ppermute | solution.py:23
  245.6 7.1 %copy-start.5 = (bf16[4,40,5120]{2,1,0:T(8,128)(2,1)}, bf16[4,40,5120]{2,1,0:T(8,128)(2,1)S(1)}, u32[]{:S(2)}) copy-start(bf16[4,40,5120]{2,1,0:T(8,128)(2,1)S(1)} %maximum_select_fusion.2) | copy-start | bytes 4915204
  245.6 98.2 %collective-permute-start.17 = (bf16[4,40,5120]{2,1,0:T(8,128)(2,1)S(1)}, bf16[4,40,5120]{2,1,0:T(8,128)(2,1)}, u32[]{:S(2)}, u32[]{:S(2)}) collective-permute-start(bf16[4,40,5120]{2,1,0:T(8,128)(2,1)S(1)} %maximum_select_fusion.2), channel_id=1, source_target_pairs={{0,4},{1,5},{2,6},{3,7},{4,0},{5,1},{6,2},{7,3},{8,12},{9,13},{10,... | collective-permute-start | bytes 4915208 | tf_op jit(solution)/shard_map/ppermute | solution.py:23
  249.3 5.8 %copy-start.7 = (f32[2,5,128,128]{2,3,1,0:T(8,128)}, f32[2,5,128,128]{2,3,1,0:T(8,128)S(1)}, u32[]{:S(2)}) copy-start(f32[2,5,128,128]{2,3,1,0:T(8,128)S(1)} %get-tuple-element.39) | copy-start | bytes 1966084
  252.7 4.2 copy-start.11
  258.6 85.2 %copy-start.6 = (bf16[4,40,5120]{2,1,0:T(8,128)(2,1)S(1)}, bf16[4,40,5120]{2,1,0:T(8,128)(2,1)}, u32[]{:S(2)}) copy-start(bf16[4,40,5120]{2,1,0:T(8,128)(2,1)} %copy-done.5) | copy-start | bytes 4915204
  258.6 105.8 %collective-permute-start.14 = (bf16[2,5,1024,128]{2,3,1,0:T(8,128)(2,1)S(1)}, bf16[2,5,1024,128]{2,3,1,0:T(8,128)(2,1)S(1)}, u32[]{:S(2)}, u32[]{:S(2)}) collective-permute-start(bf16[2,5,1024,128]{2,3,1,0:T(8,128)(2,1)S(1)} %pad_maximum_fusion.1), channel_id=1, source_target_pairs={{0,8},{1,9},{2,10},{3,11},{4,12},{5,13},{6,14},{7,15},{8,0},{9,1},... | collective-permute-start | bytes 7864328 | tf_op jit(solution)/shard_map/ppermute | solution.py:23
  261.0 94.4 %copy-start.4 = (bf16[2,5,8,16,128]{4,3,2,1,0:T(8,128)(2,1)S(1)}, bf16[2,5,8,16,128]{4,3,2,1,0:T(8,128)(2,1)}, u32[]{:S(2)}) copy-start(bf16[2,5,8,16,128]{4,3,2,1,0:T(8,128)(2,1)} %copy-done.3) | copy-start | bytes 983044
  346.2 81.0 %collective-permute-start.18 = (bf16[8,40,5120]{2,1,0:T(8,128)(2,1)S(1)}, bf16[8,40,5120]{2,1,0:T(8,128)(2,1)}, u32[]{:S(2)}, u32[]{:S(2)}) collective-permute-start(bf16[8,40,5120]{2,1,0:T(8,128)(2,1)S(1)} %maximum_select_fusion.1), channel_id=1, source_target_pairs={{0,8},{1,9},{2,10},{3,11},{4,12},{5,13},{6,14},{7,15},{8,0},{9,1},... | collective-permute-start | bytes 9830408 | tf_op jit(solution)/shard_map/ppermute | solution.py:23
  372.8 58.6 %copy-start.13 = (bf16[2,128,5,128]{1,3,2,0:T(8,128)(2,1)S(1)}, bf16[2,128,5,128]{1,3,2,0:T(8,128)(2,1)}, u32[]{:S(2)}) copy-start(bf16[2,128,5,128]{1,3,2,0:T(8,128)(2,1)} %fusion.32) | copy-start | bytes 983044
  427.2 4.5 copy-start.2
  438.3 34.2 %copy-start.20 = (s32[4]{0:T(128)S(1)}, s32[4]{0:T(128)}, u32[]{:S(2)}) copy-start(s32[4]{0:T(128)} %param.17) | copy-start | bytes 52
  438.3 36.2 %copy-start.18 = (f32[2560]{0:T(1024)S(1)}, f32[2560]{0:T(1024)}, u32[]{:S(2)}) copy-start(f32[2560]{0:T(1024)} %param.18) | copy-start | bytes 30724
  438.3 9.4 %collective-permute-start.29 = (bf16[2,16,5120]{2,1,0:T(8,128)(2,1)S(1)}, bf16[2,16,5120]{2,1,0:T(8,128)(2,1)S(1)}, u32[]{:S(2)}, u32[]{:S(2)}) collective-permute-start(bf16[2,16,5120]{2,1,0:T(8,128)(2,1)S(1)} %get-tuple-element.15), channel_id=1, source_target_pairs={{0,112},{1,113},{2,114},{3,115},{4,116},{5,117},{6,118},{7,119},{8... | collective-permute-start | bytes 983048 | tf_op jit(solution)/shard_map/ppermute | solution.py:17
  441.0 8.4 %collective-permute-start.28 = (bf16[2,16,5120]{2,1,0:T(8,128)(2,1)S(1)}, bf16[2,16,5120]{2,1,0:T(8,128)(2,1)S(1)}, u32[]{:S(2)}, u32[]{:S(2)}) collective-permute-start(bf16[2,16,5120]{2,1,0:T(8,128)(2,1)S(1)} %get-tuple-element.16), channel_id=1, source_target_pairs={{0,96},{1,97},{2,98},{3,99},{4,100},{5,101},{6,102},{7,103},{8,104... | collective-permute-start | bytes 983048 | tf_op jit(solution)/shard_map/ppermute | solution.py:17
  441.0 24.4 %collective-permute-start.27 = (bf16[2,16,5120]{2,1,0:T(8,128)(2,1)}, bf16[2,16,5120]{2,1,0:T(8,128)(2,1)}, u32[]{:S(2)}, u32[]{:S(2)}) collective-permute-start(bf16[2,16,5120]{2,1,0:T(8,128)(2,1)} %get-tuple-element.17), channel_id=1, source_target_pairs={{0,80},{1,81},{2,82},{3,83},{4,84},{5,85},{6,86},{7,87},{8,88},{9,... | collective-permute-start | bytes 983048 | tf_op jit(solution)/shard_map/ppermute | solution.py:17
  443.2 22.2 %collective-permute-start.26 = (bf16[2,16,5120]{2,1,0:T(8,128)(2,1)}, bf16[2,16,5120]{2,1,0:T(8,128)(2,1)}, u32[]{:S(2)}, u32[]{:S(2)}) collective-permute-start(bf16[2,16,5120]{2,1,0:T(8,128)(2,1)} %get-tuple-element.18), channel_id=1, source_target_pairs={{0,64},{1,65},{2,66},{3,67},{4,68},{5,69},{6,70},{7,71},{8,72},{9,... | collective-permute-start | bytes 983048 | tf_op jit(solution)/shard_map/ppermute | solution.py:17
  444.2 21.2 %collective-permute-start.25 = (bf16[2,16,5120]{2,1,0:T(8,128)(2,1)}, bf16[2,16,5120]{2,1,0:T(8,128)(2,1)}, u32[]{:S(2)}, u32[]{:S(2)}) collective-permute-start(bf16[2,16,5120]{2,1,0:T(8,128)(2,1)} %get-tuple-element.19), channel_id=1, source_target_pairs={{0,48},{1,49},{2,50},{3,51},{4,52},{5,53},{6,54},{7,55},{8,56},{9,... | collective-permute-start | bytes 983048 | tf_op jit(solution)/shard_map/ppermute | solution.py:17
  447.7 22.8 %collective-permute-start.24 = (bf16[2,16,5120]{2,1,0:T(8,128)(2,1)S(1)}, bf16[2,16,5120]{2,1,0:T(8,128)(2,1)}, u32[]{:S(2)}, u32[]{:S(2)}) collective-permute-start(bf16[2,16,5120]{2,1,0:T(8,128)(2,1)S(1)} %get-tuple-element.20), channel_id=1, source_target_pairs={{0,32},{1,33},{2,34},{3,35},{4,36},{5,37},{6,38},{7,39},{8,40},{9,... | collective-permute-start | bytes 983048 | tf_op jit(solution)/shard_map/ppermute | solution.py:17
  450.1 20.4 %collective-permute-start.23 = (bf16[2,16,5120]{2,1,0:T(8,128)(2,1)S(1)}, bf16[2,16,5120]{2,1,0:T(8,128)(2,1)}, u32[]{:S(2)}, u32[]{:S(2)}) collective-permute-start(bf16[2,16,5120]{2,1,0:T(8,128)(2,1)S(1)} %get-tuple-element.14), channel_id=1, source_target_pairs={{0,16},{1,17},{2,18},{3,19},{4,20},{5,21},{6,22},{7,23},{8,24},{9,... | collective-permute-start | bytes 983048 | tf_op jit(solution)/shard_map/ppermute | solution.py:17
  465.4 29.4 %copy-start.1 = (bf16[4,64,5120]{2,1,0:T(8,128)(2,1)S(1)}, bf16[4,64,5120]{2,1,0:T(8,128)(2,1)}, u32[]{:S(2)}) copy-start(bf16[4,64,5120]{2,1,0:T(8,128)(2,1)} %param.15) | copy-start | bytes 7864324
  (4 other events, 4.8 us)
Sparse Core Ops, SparseCore 0:
  473.9 19.2 reduce-scatter.1
where the time goes:
time: 507 us; the launch traced here: 502 us
  waiting for transfers between devices  323 us (64%)
  starting transfers between devices  70.2 us (14%)
  other arithmetic  36.3 us (7%)
  matrix products  29.5 us (6%)
  local copies, waits for them, and re-layouts  28.2 us (6%)
  between operations  14.7 us (3%)
    ppermute x16, waiting for transfers between devices, from_partner(): return lax.ppermute(value, axis, pairs)  293 us
    ppermute x14, starting transfers between devices, passed_along(): return lax.ppermute(x, axis, [(i, (i + by) % count) for i in range(count)])  36.5 us
    ppermute x16, starting transfers between devices, from_partner(): return lax.ppermute(value, axis, pairs)  33.7 us
    reduce_scatter x1, waiting for transfers between devices, shards(): lax.psum_scatter(mixture.astype(jnp.bfloat16), 'branch', scatter_dimensio...  18.7 us
    select_n x7, other arithmetic, join_rows(): jnp.where(upper_half, jnp.concatenate([got, held], axis=axis_index), jnp....  14.2 us
    ppermute x14, waiting for transfers between devices, passed_along(): return lax.ppermute(x, axis, [(i, (i + by) % count) for i in range(count)])  10.8 us
  transfers between devices with their start and end apart: 31, of which 13 were waited for; matrix products, arithmetic and copies ran while one was open for 13% of the time, Pallas kernels for 0%

commit v1 on v0

v1 whole, which is shorter than its diff:
```python
import math

import jax
import jax.numpy as jnp
from jax import lax
from jax.experimental import pallas as pl
from jax.experimental.pallas import tpu as pltpu
from jax.sharding import PartitionSpec as P

MESH = pl.DeviceIdType.MESH
BF16 = jnp.bfloat16
F32 = jnp.float32
HEAD_DIM = 128
GUIDE_UNIT = 0.125
SCORE_SCALE = HEAD_DIM**-0.5 * math.log2(math.e)


def seq_of(y, x, zh, c):
    return ((y * 4 + x) * 4 + zh) * 2 + c


def wait_for(ref, sem):
    pltpu.make_async_copy(ref, ref, sem).wait()


def send(src, dst, send_sem, recv_sem, zl, s):
    return pltpu.make_async_remote_copy(
        src_ref=src, dst_ref=dst, send_sem=send_sem, recv_sem=recv_sem, device_id=(zl, s), device_id_type=MESH
    )


def body(
    adapter,
    weight_eighths,
    q_in,
    k_in,
    v_in,
    w_in,
    down_in,
    up_in,
    out,
    q_st,
    kv_st,
    w_v,
    w_sib,
    w_st,
    w_buf,
    down_v,
    down_sib,
    down_all,
    up_v,
    up_cat,
    q_buf,
    kv,
    o_t,
    m1,
    mx,
    m2,
    lr,
    lr_got,
    lr_sum,
    p_out,
    p_got,
    lr_fin,
    in_sem,
    send_sem,
    recv_sem,
    token,
):
    s = lax.axis_index("seq")
    zl = lax.axis_index("branch")
    c = s % 2
    chip = s // 2
    zh = chip % 4
    x = (chip // 4) % 4
    y = chip // 16
    col = chip // 4
    sib = s + 1 - 2 * c
    slot_left = (y // 2) * 8 + zh * 2 + y % 2
    slot = (y // 2) * 32 + x * 8 + zh * 2 + y % 2
    (
        R_SIBW,
        R_LEFT,
        R_LEFTQ,
        R_KV,
        R_Q,
        R_AG,
        R_AGSIB,
        R_KVSIB,
        R_W,
        R_WSIB,
        R_M1,
        R_M2,
        R_LR,
        R_P,
        R_LRF,
        R_SIBD,
    ) = range(16)

    def rs(i):
        return recv_sem.at[i]

    def ss(i):
        return send_sem.at[i]

    loads = [
        pltpu.make_async_copy(w_in, w_v, in_sem.at[0]),
        pltpu.make_async_copy(down_in, down_v, in_sem.at[1]),
        pltpu.make_async_copy(k_in, kv_st.at[0], in_sem.at[2]),
        pltpu.make_async_copy(v_in, kv_st.at[1], in_sem.at[3]),
        pltpu.make_async_copy(q_in, q_st, in_sem.at[4]),
        pltpu.make_async_copy(up_in.at[:, :, pl.ds(pl.multiple_of(zl * 2560, 2560), 2560)], up_v, in_sem.at[5]),
    ]
    for load in loads:
        load.start()

    barrier = pltpu.get_barrier_semaphore()

    @pl.loop(1, 64)
    def _(i):
        pl.semaphore_signal(barrier, 1, device_id=(zl, ((chip + i) % 64) * 2 + c), device_id_type=MESH)

    pl.semaphore_signal(barrier, 1, device_id=(zl, sib), device_id_type=MESH)
    pl.semaphore_signal(barrier, 1, device_id=(1 - zl, s), device_id_type=MESH)
    for load in loads[:5]:
        load.wait()
    pl.semaphore_wait(barrier, 65)

    sib_copies = [
        send(
            w_v.at[:, pl.ds(pl.multiple_of(1280 * i + 640 * (1 - c), 128), 640)],
            w_sib.at[i],
            ss(R_SIBW),
            rs(R_SIBW),
            zl,
            sib,
        )
        for i in range(4)
    ]
    sib_copies.append(send(down_v, down_sib, ss(R_SIBD), rs(R_SIBD), zl, sib))
    for copy in sib_copies:
        copy.start()

    def left_copy(i):
        y2 = i // 4
        z2 = i % 4
        head = 5 * (2 * y2 + z2 // 2) + 2
        lanes = pl.ds(pl.multiple_of(head * 128, 128), 128)
        pair = z2 % 2
        return (
            (kv_st.at[:, pair, :, lanes], kv.at[1, 0, :, x * 16 + slot_left], R_LEFT),
            (q_st.at[pair, :, lanes], q_buf.at[64 + slot_left], R_LEFTQ),
        )

    @pl.loop(1, 16)
    def _(j):
        i = (y * 4 + zh + j) % 16
        for src, dst, n in left_copy(i):
            send(src, dst, ss(n), rs(n), zl, seq_of(i // 4, x, i % 4, c)).start()

    for src, dst, n in left_copy(y * 4 + zh):
        pltpu.make_async_copy(src, dst, rs(n)).start()

    def main_copy(i):
        y2 = i // 16
        x2 = (i // 4) % 4
        z2 = i % 4
        head = 5 * (2 * y2 + x2 // 2) + 3 * (x2 % 2) + z2 // 2
        lanes = pl.ds(pl.multiple_of(head * 128, 128), 128)
        pair = z2 % 2
        return (
            (kv_st.at[:, pair, :, lanes], kv.at[0, 0, :, slot], R_KV),
            (q_st.at[pair, :, lanes], q_buf.at[slot], R_Q),
        )

    for part in range(2):

        @pl.loop(1, 64)
        def _(j):
            i = (chip + j) % 64
            src, dst, n = main_copy(i)[part]
            send(src, dst, ss(n), rs(n), zl, i * 2 + c).start()

        src, dst, n = main_copy(chip)[part]
        pltpu.make_async_copy(src, dst, rs(n)).start()

    wait_for(w_sib, rs(R_SIBW))
    wait_for(down_sib, rs(R_SIBD))
    pl.semaphore_signal(token, 1, device_id=(1 - zl, s), device_id_type=MESH)

    def joined(own, other):
        first = jnp.where(c == 0, own, other)
        second = jnp.where(c == 0, other, own)
        return jnp.concatenate([first, second], axis=0).astype(BF16)

    for i in range(4):
        own = w_v[:, pl.ds(pl.multiple_of(1280 * i + 640 * c, 128), 640)].astype(F32)
        w_st[i] = joined(own, w_sib[i].astype(F32))

    def w_copy(i):
        return w_st.at[i % 4], w_buf.at[c, col]

    @pl.loop(1, 16)
    def _(j):
        i = (col + j) % 16
        src, dst = w_copy(i)
        send(src, dst, ss(R_W), rs(R_W), zl, seq_of(i // 4, i % 4, zh, c)).start()

    src, dst = w_copy(col)
    pltpu.make_async_copy(src, dst, rs(R_W)).start()
    for i in range(4):
        down_all[i] = joined(down_v[i].astype(F32), down_sib[i].astype(F32))
    loads[5].wait()
    for i in range(4):
        up_cat[64 * i : 64 * (i + 1), :] = up_v[adapter[i]]

    slab = kv.at[1, 0, :, pl.ds(x * 16, 16)]
    wait_for(slab, rs(R_LEFT))
    wait_for(q_buf.at[pl.ds(64, 16)], rs(R_LEFTQ))

    def ag_copy(j):
        return send(slab, slab, ss(R_AG), rs(R_AG), zl, seq_of(y, (x + j) % 4, zh, c))

    for j in range(1, 4):
        ag_copy(j).start()
    wait_for(kv.at[1, 0, :, pl.ds(0, 48)], rs(R_AG))
    ag_sib = send(kv.at[1, 0], kv.at[1, 1], ss(R_AGSIB), rs(R_AGSIB), zl, sib)
    ag_sib.start()
    wait_for(kv.at[0, 0], rs(R_KV))
    kv_sib = send(kv.at[0, 0], kv.at[0, 1], ss(R_KVSIB), rs(R_KVSIB), zl, sib)
    kv_sib.start()
    wait_for(q_buf.at[pl.ds(0, 64)], rs(R_Q))
    wait_for(kv.at[1, 1], rs(R_AGSIB))
    wait_for(kv.at[0, 1], rs(R_KVSIB))

    def attend(tile, which):
        q = q_buf[pl.ds(tile * 16, 16)].reshape(256, 128)
        scores = [
            lax.dot_general(
                q, kv[which, half, 0].reshape(1024, 128), (((1,), (1,)), ((), ())), preferred_element_type=F32
            )
            * SCORE_SCALE
            for half in range(2)
        ]
        top = jnp.maximum(
            jnp.max(scores[0], axis=1, keepdims=True), jnp.max(scores[1], axis=1, keepdims=True)
        )
        total = 0.0
        mixed = 0.0
        for half in range(2):
            weights = jnp.exp2(scores[half] - top)
            total = total + jnp.sum(weights, axis=1, keepdims=True)
            mixed = mixed + jnp.dot(
                weights.astype(BF16), kv[which, half, 1].reshape(1024, 128), preferred_element_type=F32
            )
        o_t[:, pl.ds(pl.multiple_of(tile * 256, 256), 256)] = jnp.transpose(mixed / total).astype(BF16)

    unit0 = 12 * (x % 2) * (zh // 2) + 4 * (x % 2) * (1 - zh // 2) + 8 * (1 - x % 2) * (zh // 2)
    pair_all = 2 * zl + zh % 2

    def m1_copy(i):
        u = i % 8
        core2 = i // 8
        place = unit0 + u
        z2 = place // 5
        row = pl.multiple_of((place % 5) * 16, 16)
        src = o_t.at[pl.ds(pl.multiple_of(u * 16, 16), 16), pl.ds(pl.multiple_of(core2 * 512, 512), 512)]
        dst = m1.at[pair_all, pl.ds(row, 16)]
        return src, dst, z2, core2

    def m1_left_copy(i):
        odd = i % 2
        core2 = i // 2
        src = o_t.at[
            pl.ds(pl.multiple_of(odd * 64, 16), 64), pl.ds(pl.multiple_of(1024 + core2 * 128, 128), 128)
        ]
        dst = m1.at[
            pair_all, pl.ds(pl.multiple_of(16 * (1 - odd), 16), 64), pl.ds(pl.multiple_of(x * 128, 128), 128)
        ]
        return src, dst, 2 * (zh // 2) + odd, 3 * (1 - odd), core2

    def m1_start(i):
        src, dst, z2, core2 = m1_copy(i)
        mine = jnp.logical_and(jnp.logical_and(z2 == zh, c == zl), core2 == c)

        @pl.when(mine)
        def _():
            pltpu.make_async_copy(src, dst, rs(R_M1)).start()

        @pl.when(jnp.logical_not(mine))
        def _():
            send(src, dst, ss(R_M1), rs(R_M1), c, seq_of(y, x, z2, core2)).start()

    def m1_wait_send(i):
        src, dst, z2, core2 = m1_copy(i)
        mine = jnp.logical_and(jnp.logical_and(z2 == zh, c == zl), core2 == c)

        @pl.when(jnp.logical_not(mine))
        def _():
            send(src, dst, ss(R_M1), rs(R_M1), c, seq_of(y, x, z2, core2)).wait_send()

    def left_mine(x2, z2, core2):
        here = jnp.logical_and(x2 == x, z2 == zh)
        return jnp.logical_and(here, jnp.logical_and(c == zl, core2 == c))

    def m1_left_start(i):
        src, dst, x2, z2, core2 = m1_left_copy(i)
        mine = left_mine(x2, z2, core2)

        @pl.when(mine)
        def _():
            pltpu.make_async_copy(src, dst, rs(R_M1)).start()

        @pl.when(jnp.logical_not(mine))
        def _():
            send(src, dst, ss(R_M1), rs(R_M1), c, seq_of(y, x2, z2, core2)).start()

    def m1_left_wait_send(i):
        src, dst, x2, z2, core2 = m1_left_copy(i)

        @pl.when(jnp.logical_not(left_mine(x2, z2, core2)))
        def _():
            send(src, dst, ss(R_M1), rs(R_M1), c, seq_of(y, x2, z2, core2)).wait_send()

    pl.semaphore_wait(token, 1)

    @pl.loop(0, 2)
    def _(core2):
        @pl.loop(0, 2)
        def _(j):
            attend(core2 * 2 + j, 0)

        @pl.loop(0, 8)
        def _(u):
            m1_start(core2 * 8 + u)

    attend(4, 1)

    @pl.loop(0, 4)
    def _(i):
        m1_left_start(i)

    wait_for(w_buf.at[0], rs(R_W))
    w_fwd = send(w_buf.at[c], w_buf.at[c], ss(R_WSIB), rs(R_WSIB), zl, sib)
    w_fwd.start()

    wait_for(m1, rs(R_M1))
    guide = [weight_eighths[i].astype(F32) * GUIDE_UNIT for i in range(4)]
    total = m1[0].astype(F32) * guide[0]
    for i in range(1, 4):
        total = total + m1[i].astype(F32) * guide[i]
    mx[...] = total.astype(BF16)

    def m2_copy(i):
        src = mx.at[:, pl.ds(pl.multiple_of((i // 4) * 128, 128), 128)]
        return src, m2.at[col]

    @pl.loop(1, 16)
    def _(j):
        i = (col + j) % 16
        src, dst = m2_copy(i)
        send(src, dst, ss(R_M2), rs(R_M2), zl, seq_of(i // 4, i % 4, zh, c)).start()

    src, dst = m2_copy(col)
    pltpu.make_async_copy(src, dst, rs(R_M2)).start()

    ranks = jnp.concatenate(
        [
            lax.dot_general(
                down_all[adapter[i]], m1[i], (((0,), (0,)), ((), ())), preferred_element_type=F32
            )
            * guide[i]
            for i in range(4)
        ],
        axis=0,
    )
    lr[...] = jnp.transpose(ranks).astype(BF16)

    def lr_copy(i):
        src = lr.at[pl.ds(pl.multiple_of(i * 32, 32), 32)]
        return src, lr_got.at[col]

    @pl.loop(1, 16)
    def _(j):
        i = (col + j) % 16
        src, dst = lr_copy(i)
        send(src, dst, ss(R_LR), rs(R_LR), zl, seq_of(i // 4, i % 4, zh, c)).start()

    src, dst = lr_copy(col)
    pltpu.make_async_copy(src, dst, rs(R_LR)).start()

    wait_for(w_buf.at[0], rs(R_WSIB))
    wait_for(m2, rs(R_M2))
    rows = jnp.transpose(m2[...].reshape(1280, 128).astype(F32)).astype(BF16)
    for half in range(2):
        p_out[:, 640 * half : 640 * (half + 1)] = jnp.dot(
            rows, w_buf[half].reshape(1280, 640), preferred_element_type=F32
        ).astype(BF16)

    def p_copy(i):
        z2 = i // 2
        y2 = 2 * c + i % 2
        src = p_out.at[pl.ds(pl.multiple_of(i * 16, 16), 16)]
        dst = p_got.at[zh, :, pl.ds(pl.multiple_of((x % 2) * 1280, 1280), 1280)]
        here = jnp.logical_and(jnp.logical_and(y2 == y, y == x), jnp.logical_and(z2 == zh, x // 2 == zl))
        return src, dst, seq_of(y2, y, z2, zl), jnp.logical_and(here, c == zl)

    @pl.loop(0, 8)
    def _(i):
        src, dst, to, mine = p_copy(i)

        @pl.when(mine)
        def _():
            pltpu.make_async_copy(src, dst, rs(R_P)).start()

        @pl.when(jnp.logical_not(mine))
        def _():
            send(src, dst, ss(R_P), rs(R_P), x // 2, to).start()

    wait_for(lr_got, rs(R_LR))
    low = lr_got[0].astype(F32)
    for i in range(1, 16):
        low = low + lr_got[i].astype(F32)
    lr_sum[...] = low.astype(BF16)

    def lrf_copy(i):
        y2 = 2 * c + i // 2
        zl2 = i % 2
        src = lr_sum.at[pl.ds(pl.multiple_of((i // 2) * 16, 16), 16)]
        dst = lr_fin.at[zh]
        here = jnp.logical_and(jnp.logical_and(y2 == y, y == x), jnp.logical_and(x == zh, zl2 == zl))
        return src, dst, zl2, seq_of(y2, y, x, zl), jnp.logical_and(here, c == zl)

    @pl.loop(0, 4)
    def _(i):
        src, dst, zl2, to, mine = lrf_copy(i)

        @pl.when(mine)
        def _():
            pltpu.make_async_copy(src, dst, rs(R_LRF)).start()

        @pl.when(jnp.logical_not(mine))
        def _():
            send(src, dst, ss(R_LRF), rs(R_LRF), zl2, to).start()

    wait_for(lr_fin, rs(R_LRF))
    low = lr_fin[0].astype(F32)
    for i in range(1, 4):
        low = low + lr_fin[i].astype(F32)
    adapted = jnp.dot(low.astype(BF16), up_cat[...], preferred_element_type=F32)
    wait_for(p_got, rs(R_P))
    for i in range(4):
        adapted = adapted + p_got[i].astype(F32)
    out[...] = adapted

    for copy in sib_copies:
        copy.wait_send()
    wait_for(kv.at[1, 0, :, pl.ds(0, 15)], ss(R_LEFT))
    wait_for(q_buf.at[pl.ds(0, 15)], ss(R_LEFTQ))
    wait_for(kv.at[0, 0, :, pl.ds(0, 63)], ss(R_KV))
    wait_for(q_buf.at[pl.ds(0, 63)], ss(R_Q))
    wait_for(w_buf.at[0, pl.ds(0, 15)], ss(R_W))
    wait_for(kv.at[1, 0, :, pl.ds(0, 48)], ss(R_AG))
    ag_sib.wait_send()
    kv_sib.wait_send()
    w_fwd.wait_send()

    @pl.loop(0, 16)
    def _(i):
        m1_wait_send(i)

    @pl.loop(0, 4)
    def _(i):
        m1_left_wait_send(i)

    wait_for(m2.at[pl.ds(0, 15)], ss(R_M2))
    wait_for(lr_got.at[pl.ds(0, 15)], ss(R_LR))

    @pl.loop(0, 8)
    def _(i):
        src, dst, to, mine = p_copy(i)

        @pl.when(jnp.logical_not(mine))
        def _():
            send(src, dst, ss(R_P), rs(R_P), x // 2, to).wait_send()

    @pl.loop(0, 4)
    def _(i):
        src, dst, zl2, to, mine = lrf_copy(i)

        @pl.when(jnp.logical_not(mine))
        def _():
            send(src, dst, ss(R_LRF), rs(R_LRF), zl2, to).wait_send()


def shards(q, k, v, w, down, up, adapter, weight_eighths, gate_offset, timestep):
    whole = pl.BlockSpec(memory_space=pl.ANY)
    smem = pl.BlockSpec(memory_space=pltpu.SMEM)
    vm = pltpu.VMEM
    mixture = pl.pallas_call(
        body,
        out_shape=jax.ShapeDtypeStruct((16, 2560), F32),
        in_specs=[smem, smem] + [whole] * 6,
        out_specs=pl.BlockSpec(memory_space=pltpu.VMEM),
        scratch_shapes=[
            vm((2, 16, 5120), BF16),
            vm((2, 2, 16, 5120), BF16),
            vm((40, 5120), BF16),
            vm((4, 40, 640), BF16),
            vm((4, 80, 640), BF16),
            vm((2, 16, 80, 640), BF16),
            vm((4, 40, 64), BF16),
            vm((4, 40, 64), BF16),
            vm((4, 80, 64), BF16),
            vm((4, 64, 2560), BF16),
            vm((256, 2560), BF16),
            vm((80, 16, 128), BF16),
            vm((2, 2, 2, 64, 16, 128), BF16),
            vm((128, 1280), BF16),
            vm((4, 80, 512), BF16),
            vm((80, 512), BF16),
            vm((16, 80, 128), BF16),
            vm((512, 256), BF16),
            vm((16, 32, 256), BF16),
            vm((32, 256), BF16),
            vm((128, 1280), BF16),
            vm((4, 16, 2560), BF16),
            vm((4, 16, 256), BF16),
            pltpu.SemaphoreType.DMA((6,)),
            pltpu.SemaphoreType.DMA((16,)),
            pltpu.SemaphoreType.DMA((16,)),
            pltpu.SemaphoreType.REGULAR,
        ],
        compiler_params=pltpu.CompilerParams(
            collective_id=0, has_side_effects=True, vmem_limit_bytes=48 * 2**20
        ),
        name="guided_attention",
    )(adapter, weight_eighths, q, k, v, w, down, up)

    columns = lax.axis_index("branch") * 2560 + jnp.arange(2560, dtype=jnp.int32)
    frequency = jnp.exp((columns % 2560).astype(F32) * (-math.log(10000.0) / 2560))
    angles = timestep.astype(F32)[0] * frequency
    gate_row = gate_offset + jnp.where(columns < 2560, jnp.cos(angles), jnp.sin(angles))
    return (mixture * gate_row[None, :]).astype(BF16)


def solution(mesh):
    placed = (
        P("branch", "seq", None),
        P("branch", "seq", None),
        P("branch", "seq", None),
        P("seq", None),
        P(None, "seq", None),
        P(),
        P(),
        P(),
        P("branch"),
        P(),
    )
    return jax.shard_map(
        shards, mesh=mesh, in_specs=placed, out_specs=P("seq", "branch"), check_vma=False
    )
```

time: 507 us -> 122 us (0.24)
  waiting for transfers between devices: 323 us -> 0 us
  Pallas kernels: 0 us -> 111 us
  starting transfers between devices: 70.2 us -> 0 us
  other arithmetic: 36.3 us -> 1.43 us
  matrix products: 29.5 us -> 0 us
  local copies, waits for them, and re-layouts: 28.2 us -> 7.74 us
  between operations: 14.7 us -> 0.68 us
    ppermute x30 -> x0, waiting for transfers between devices: 304 us -> none  [the longest x16 293 us: from_partner(): return lax.ppermute(value, axis, pairs)]
    pallas_call x0 -> x1, Pallas kernels: none -> 111 us  [shards(): pl.pallas_call(body, out_shape=jax.ShapeDtypeStruct((16, 2560), F32), in_...]
    ppermute x30 -> x0, starting transfers between devices: 70.2 us -> none  [the longest x14 36.5 us: passed_along(): return lax.ppermute(x, axis, [(i, (i + by) % count) for i in range(count)])]
    dot_general x15 -> x0, matrix products: 29.5 us -> none  [the longest x5 7.24 us: fold_keys(): jnp.einsum('bhqk,bhkd->bhqd', weights.astype(jnp.bfloat16), value_piece,...]
    reduce_scatter x1 -> x0, waiting for transfers between devices: 18.7 us -> none  [shards(): lax.psum_scatter(mixture.astype(jnp.bfloat16), 'branch', scatter_dimensio...]
    select_n x9 -> x0, other arithmetic: 15.5 us -> none  [the longest x7 14.2 us: join_rows(): jnp.where(upper_half, jnp.concatenate([got, held], axis=axis_index), jnp....]
    concatenate x6 -> x0, other arithmetic: 11.9 us -> none  [the longest x3 6 us: shards(): value_held = jnp.concatenate([value_held, value_got], axis=2)]
  transfers between devices with their start and end apart: 31 -> 0, of which waited for: 13 -> 0; matrix products, arithmetic and copies ran while one was open for 13% -> 0% of each run, Pallas kernels for 0% -> 0%
where the time goes in v1:
time: 122 us; the launch traced here: 121 us
  Pallas kernels  111 us (91%)
  local copies, waits for them, and re-layouts  7.74 us (6%)
  other arithmetic  1.43 us (1%)
    pallas_call x1, Pallas kernels, shards(): pl.pallas_call(body, out_shape=jax.ShapeDtypeStruct((16, 2560), F32), in_...  111 us
    unnamed x16, local copies, waits for them, and re-layouts  7.74 us

profile of v1, /device:TPU:1, one launch (start us, length us, event | category | flops | bytes accessed | tf_op | source)
XLA Modules:
  0.0 120.6 jit_solution(10740492952464691624)
XLA Ops:
  0.7 0.8 select_add_fusion
  1.4 0.0 copy-start
  1.5 1.7 %copy-done = bf16[4,64,5120]{2,1,0:T(8,128)(2,1)S(1)} copy-done((bf16[4,64,5120]{2,1,0:T(8,128)(2,1)S(1)}, bf16[4,64,5120]{2,1,0:T(8,128)(2,1)}, u32[]{:S(2)}) %copy-start) | copy-done | bytes 2621464
  3.2 0.0 copy-start.1
  3.2 1.0 copy-done.1
  4.2 0.0 copy-start.2
  4.2 1.0 copy-done.2
  5.2 0.0 copy-start.3
  5.2 1.0 copy-done.3
  6.1 0.0 copy-start.4
  6.1 1.0 copy-done.4
  7.1 0.0 copy-start.5
  7.1 0.8 copy-done.5
  7.9 0.0 copy-start.6
  7.9 0.7 copy-done.6
  8.5 0.0 copy-start.7
  8.5 0.7 copy-done.7
  9.2 110.7 %guided_attention.1 = f32[16,2560]{1,0:T(8,128)S(1)} custom-call(s32[4]{0:T(128)S(1)} %copy-done.6, s32[4]{0:T(128)S(1)} %copy-done.7, bf16[2,16,5120]{2,1,0:T(8,128)(2,1)S(1)} %copy-done.2, bf16[2,16,5120]{2,1,0:T(8,128)(2,1)S(1)} %copy-done.3, bf16[2,16,5120]{2,1,0:T(8,128)(2,1)S(1)} %copy-done.4, bf16[40,5120]{1,0:T(8,128)(2,1)S(1)} %copy-done.1, ...), custom_call_target="tpu_custom_call" | custom-call | tf_op jit(solution)/shard_map/guided_attention/pallas_call | solution.py:500
  119.9 0.7 multiply_convert_fusion
Async XLA Ops:
  1.4 1.7 %copy-start = (bf16[4,64,5120]{2,1,0:T(8,128)(2,1)S(1)}, bf16[4,64,5120]{2,1,0:T(8,128)(2,1)}, u32[]{:S(2)}) copy-start(bf16[4,64,5120]{2,1,0:T(8,128)(2,1)} %up_in.1) | copy-start | bytes 7864324
  3.2 1.0 copy-start.1
  4.2 1.0 copy-start.2
  5.2 1.0 copy-start.3
  6.1 1.0 copy-start.4
  7.1 0.8 copy-start.5
  7.9 0.7 copy-start.6
  8.5 0.7 copy-start.7

commit v2 on v1

--- a/solution.py
+++ b/solution.py
@@ -76,8 +76,8 @@
     y = chip // 16
     col = chip // 4
     sib = s + 1 - 2 * c
-    slot_left = (y // 2) * 8 + zh * 2 + y % 2
-    slot = (y // 2) * 32 + x * 8 + zh * 2 + y % 2
+    slot_left = (x // 2) * 8 + (x % 2) * 4 + zh
+    slot = (x // 2) * 32 + y * 8 + (x % 2) * 4 + zh
     (
         R_SIBW,
         R_LEFT,
@@ -95,7 +95,8 @@
         R_P,
         R_LRF,
         R_SIBD,
-    ) = range(16)
+        R_WX,
+    ) = range(17)
 
     def rs(i):
         return recv_sem.at[i]
@@ -141,6 +142,23 @@
     for copy in sib_copies:
         copy.start()
 
+    wait_for(w_sib, rs(R_SIBW))
+    wait_for(down_sib, rs(R_SIBD))
+    pl.semaphore_signal(token, 1, device_id=(1 - zl, s), device_id_type=MESH)
+
+    def joined(own, other):
+        first = jnp.where(c == 0, own, other)
+        second = jnp.where(c == 0, other, own)
+        return jnp.concatenate([first, second], axis=0).astype(BF16)
+
+    for i in range(4):
+        own = w_v[:, pl.ds(pl.multiple_of(1280 * i + 640 * c, 128), 640)].astype(F32)
+        w_st[i] = joined(own, w_sib[i].astype(F32))
+    for j in range(1, 4):
+        i = (x + j) % 4
+        send(w_st.at[i], w_buf.at[c, col], ss(R_WX), rs(R_WX), zl, seq_of(y, i, zh, c)).start()
+    pltpu.make_async_copy(w_st.at[x], w_buf.at[c, col], rs(R_WX)).start()
+
     def left_copy(i):
         y2 = i // 4
         z2 = i % 4
@@ -148,18 +166,28 @@
         lanes = pl.ds(pl.multiple_of(head * 128, 128), 128)
         pair = z2 % 2
         return (
-            (kv_st.at[:, pair, :, lanes], kv.at[1, 0, :, x * 16 + slot_left], R_LEFT),
+            (kv_st.at[:, pair, :, lanes], kv.at[1, 0, :, x * 16 + y * 4 + zh], R_LEFT),
             (q_st.at[pair, :, lanes], q_buf.at[64 + slot_left], R_LEFTQ),
         )
 
     @pl.loop(1, 16)
     def _(j):
         i = (y * 4 + zh + j) % 16
-        for src, dst, n in left_copy(i):
-            send(src, dst, ss(n), rs(n), zl, seq_of(i // 4, x, i % 4, c)).start()
-
-    for src, dst, n in left_copy(y * 4 + zh):
-        pltpu.make_async_copy(src, dst, rs(n)).start()
+        (src, dst, n), (src_q, dst_q, n_q) = left_copy(i)
+        send(src, dst, ss(n), rs(n), zl, seq_of(i // 4, x, i % 4, c)).start()
+        send(src_q, dst_q, ss(n_q), rs(n_q), zl, seq_of(i // 4, y, i % 4, c)).start()
+
+    (src, dst, n), (src_q, dst_q, n_q) = left_copy(y * 4 + zh)
+    pltpu.make_async_copy(src, dst, rs(n)).start()
+    left_q_far = send(src_q, dst_q, ss(n_q), rs(n_q), zl, seq_of(y, y, zh, c))
+
+    @pl.when(x == y)
+    def _():
+        pltpu.make_async_copy(src_q, dst_q, rs(n_q)).start()
+
+    @pl.when(x != y)
+    def _():
+        left_q_far.start()
 
     def main_copy(i):
         y2 = i // 16
@@ -173,8 +201,7 @@
             (q_st.at[pair, :, lanes], q_buf.at[slot], R_Q),
         )
 
-    for part in range(2):
-
+    def main_sends(part):
         @pl.loop(1, 64)
         def _(j):
             i = (chip + j) % 64
@@ -184,30 +211,12 @@
         src, dst, n = main_copy(chip)[part]
         pltpu.make_async_copy(src, dst, rs(n)).start()
 
-    wait_for(w_sib, rs(R_SIBW))
-    wait_for(down_sib, rs(R_SIBD))
-    pl.semaphore_signal(token, 1, device_id=(1 - zl, s), device_id_type=MESH)
-
-    def joined(own, other):
-        first = jnp.where(c == 0, own, other)
-        second = jnp.where(c == 0, other, own)
-        return jnp.concatenate([first, second], axis=0).astype(BF16)
-
-    for i in range(4):
-        own = w_v[:, pl.ds(pl.multiple_of(1280 * i + 640 * c, 128), 640)].astype(F32)
-        w_st[i] = joined(own, w_sib[i].astype(F32))
-
-    def w_copy(i):
-        return w_st.at[i % 4], w_buf.at[c, col]
-
-    @pl.loop(1, 16)
-    def _(j):
-        i = (col + j) % 16
-        src, dst = w_copy(i)
-        send(src, dst, ss(R_W), rs(R_W), zl, seq_of(i // 4, i % 4, zh, c)).start()
-
-    src, dst = w_copy(col)
-    pltpu.make_async_copy(src, dst, rs(R_W)).start()
+    main_sends(0)
+    w_slab = w_buf.at[c, pl.ds(y * 4, 4)]
+    wait_for(w_slab, rs(R_WX))
+    for j in range(1, 4):
+        send(w_slab, w_slab, ss(R_W), rs(R_W), zl, seq_of((y + j) % 4, x, zh, c)).start()
+    main_sends(1)
     for i in range(4):
         down_all[i] = joined(down_v[i].astype(F32), down_sib[i].astype(F32))
     loads[5].wait()
@@ -340,7 +349,7 @@
     def _(i):
         m1_left_start(i)
 
-    wait_for(w_buf.at[0], rs(R_W))
+    wait_for(w_buf.at[0, pl.ds(0, 12)], rs(R_W))
     w_fwd = send(w_buf.at[c], w_buf.at[c], ss(R_WSIB), rs(R_WSIB), zl, sib)
     w_fwd.start()
 
@@ -398,12 +407,12 @@
         ).astype(BF16)
 
     def p_copy(i):
-        z2 = i // 2
-        y2 = 2 * c + i % 2
+        x2 = 2 * c + i // 4
+        z2 = i % 4
         src = p_out.at[pl.ds(pl.multiple_of(i * 16, 16), 16)]
         dst = p_got.at[zh, :, pl.ds(pl.multiple_of((x % 2) * 1280, 1280), 1280)]
-        here = jnp.logical_and(jnp.logical_and(y2 == y, y == x), jnp.logical_and(z2 == zh, x // 2 == zl))
-        return src, dst, seq_of(y2, y, z2, zl), jnp.logical_and(here, c == zl)
+        here = jnp.logical_and(jnp.logical_and(x2 == x, z2 == zh), x // 2 == zl)
+        return src, dst, seq_of(y, x2, z2, zl), jnp.logical_and(here, c == zl)
 
     @pl.loop(0, 8)
     def _(i):
@@ -424,12 +433,13 @@
     lr_sum[...] = low.astype(BF16)
 
     def lrf_copy(i):
-        y2 = 2 * c + i // 2
+        x2 = 2 * c + x // 2
+        z2 = 2 * (x % 2) + i // 2
         zl2 = i % 2
         src = lr_sum.at[pl.ds(pl.multiple_of((i // 2) * 16, 16), 16)]
         dst = lr_fin.at[zh]
-        here = jnp.logical_and(jnp.logical_and(y2 == y, y == x), jnp.logical_and(x == zh, zl2 == zl))
-        return src, dst, zl2, seq_of(y2, y, x, zl), jnp.logical_and(here, c == zl)
+        here = jnp.logical_and(jnp.logical_and(x2 == x, z2 == zh), zl2 == zl)
+        return src, dst, zl2, seq_of(y, x2, z2, zl), jnp.logical_and(here, c == zl)
 
     @pl.loop(0, 4)
     def _(i):
@@ -457,9 +467,15 @@
         copy.wait_send()
     wait_for(kv.at[1, 0, :, pl.ds(0, 15)], ss(R_LEFT))
     wait_for(q_buf.at[pl.ds(0, 15)], ss(R_LEFTQ))
+
+    @pl.when(x != y)
+    def _():
+        left_q_far.wait_send()
+
     wait_for(kv.at[0, 0, :, pl.ds(0, 63)], ss(R_KV))
     wait_for(q_buf.at[pl.ds(0, 63)], ss(R_Q))
-    wait_for(w_buf.at[0, pl.ds(0, 15)], ss(R_W))
+    wait_for(w_buf.at[0, pl.ds(0, 3)], ss(R_WX))
+    wait_for(w_buf.at[0, pl.ds(0, 12)], ss(R_W))
     wait_for(kv.at[1, 0, :, pl.ds(0, 48)], ss(R_AG))
     ag_sib.wait_send()
     kv_sib.wait_send()
@@ -527,12 +543,12 @@
             vm((4, 16, 2560), BF16),
             vm((4, 16, 256), BF16),
             pltpu.SemaphoreType.DMA((6,)),
-            pltpu.SemaphoreType.DMA((16,)),
-            pltpu.SemaphoreType.DMA((16,)),
+            pltpu.SemaphoreType.DMA((17,)),
+            pltpu.SemaphoreType.DMA((17,)),
             pltpu.SemaphoreType.REGULAR,
         ],
         compiler_params=pltpu.CompilerParams(
-            collective_id=0, has_side_effects=True, vmem_limit_bytes=48 * 2**20
+            collective_id=0, has_side_effects=True, vmem_limit_bytes=62 * 2**20
         ),
         name="guided_attention",
     )(adapter, weight_eighths, q, k, v, w, down, up)

time: 122 us -> 91.2 us (0.75); the launches traced: 121 us -> 91 us
  Pallas kernels: 111 us -> 88 us
  local copies, waits for them, and re-layouts: 7.74 us -> 0 us
    pallas_call x1, Pallas kernels: 111 us -> 88 us  [shards(): pl.pallas_call(body, out_shape=jax.ShapeDtypeStruct((16, 2560), F32), in_...]
    unnamed x16 -> x0, local copies, waits for them, and re-layouts: 7.74 us -> none
where the time goes in v2:
time: 91.2 us; the launch traced here: 91 us
  Pallas kernels  88 us (96%)
  other arithmetic  2.35 us (3%)
    pallas_call x1, Pallas kernels, shards(): pl.pallas_call(body, out_shape=jax.ShapeDtypeStruct((16, 2560), F32), in_...  88 us

profile of v2, /device:TPU:1, one launch (start us, length us, event | category | flops | bytes accessed | tf_op | source)
XLA Modules:
  0.0 91.0 jit_solution(16441124823591475819)
XLA Ops:
  0.7 0.8 select_add_fusion
  1.4 88.0 %guided_attention.1 = f32[16,2560]{1,0:T(8,128)} custom-call(s32[4]{0:T(128)} %adapter.1, s32[4]{0:T(128)} %weight_eighths.1, bf16[2,16,5120]{2,1,0:T(8,128)(2,1)} %q_in.1, bf16[2,16,5120]{2,1,0:T(8,128)(2,1)} %k_in.1, bf16[2,16,5120]{2,1,0:T(8,128)(2,1)} %v_in.1, bf16[40,5120]{1,0:T(8,128)(2,1)} %w_in.1, bf16[4,40,64]{2,1,0:T(8,128)(2,1)} %down_in.1, ...), custom_call_target="tpu_custom_call" | custom-call | tf_op jit(solution)/shard_map/guided_attention/pallas_call | solution.py:516
  89.5 1.6 %multiply_convert_fusion = bf16[16,2560]{1,0:T(8,128)(2,1)} fusion(f32[16,2560]{1,0:T(8,128)} %guided_attention.1, f32[2560]{0:T(1024)S(1)} %select_add_fusion), kind=kLoop, calls=%fused_computation | loop fusion | flops 81920 | bytes 256000 | tf_op jit(solution)/shard_map/convert_element_type | solution.py:560

commit v3 on v2

--- a/solution.py
+++ b/solution.py
@@ -39,8 +39,7 @@
     down_in,
     up_in,
     out,
-    q_st,
-    kv_st,
+    qkv_st,
     w_v,
     w_sib,
     w_st,
@@ -50,8 +49,11 @@
     down_all,
     up_v,
     up_cat,
-    q_buf,
-    kv,
+    main,
+    main_sib,
+    left_q,
+    left,
+    left_sib,
     o_t,
     m1,
     mx,
@@ -82,8 +84,7 @@
         R_SIBW,
         R_LEFT,
         R_LEFTQ,
-        R_KV,
-        R_Q,
+        R_MAIN,
         R_AG,
         R_AGSIB,
         R_KVSIB,
@@ -96,7 +97,7 @@
         R_LRF,
         R_SIBD,
         R_WX,
-    ) = range(17)
+    ) = range(16)
 
     def rs(i):
         return recv_sem.at[i]
@@ -107,9 +108,9 @@
     loads = [
         pltpu.make_async_copy(w_in, w_v, in_sem.at[0]),
         pltpu.make_async_copy(down_in, down_v, in_sem.at[1]),
-        pltpu.make_async_copy(k_in, kv_st.at[0], in_sem.at[2]),
-        pltpu.make_async_copy(v_in, kv_st.at[1], in_sem.at[3]),
-        pltpu.make_async_copy(q_in, q_st, in_sem.at[4]),
+        pltpu.make_async_copy(k_in, qkv_st.at[1], in_sem.at[2]),
+        pltpu.make_async_copy(v_in, qkv_st.at[2], in_sem.at[3]),
+        pltpu.make_async_copy(q_in, qkv_st.at[0], in_sem.at[4]),
         pltpu.make_async_copy(up_in.at[:, :, pl.ds(pl.multiple_of(zl * 2560, 2560), 2560)], up_v, in_sem.at[5]),
     ]
     for load in loads:
@@ -166,8 +167,8 @@
         lanes = pl.ds(pl.multiple_of(head * 128, 128), 128)
         pair = z2 % 2
         return (
-            (kv_st.at[:, pair, :, lanes], kv.at[1, 0, :, x * 16 + y * 4 + zh], R_LEFT),
-            (q_st.at[pair, :, lanes], q_buf.at[64 + slot_left], R_LEFTQ),
+            (qkv_st.at[pl.ds(1, 2), pair, :, lanes], left.at[:, x * 16 + y * 4 + zh], R_LEFT),
+            (qkv_st.at[0, pair, :, lanes], left_q.at[slot_left], R_LEFTQ),
         )
 
     @pl.loop(1, 16)
@@ -196,60 +197,50 @@
         head = 5 * (2 * y2 + x2 // 2) + 3 * (x2 % 2) + z2 // 2
         lanes = pl.ds(pl.multiple_of(head * 128, 128), 128)
         pair = z2 % 2
-        return (
-            (kv_st.at[:, pair, :, lanes], kv.at[0, 0, :, slot], R_KV),
-            (q_st.at[pair, :, lanes], q_buf.at[slot], R_Q),
-        )
-
-    def main_sends(part):
-        @pl.loop(1, 64)
-        def _(j):
-            i = (chip + j) % 64
-            src, dst, n = main_copy(i)[part]
-            send(src, dst, ss(n), rs(n), zl, i * 2 + c).start()
-
-        src, dst, n = main_copy(chip)[part]
-        pltpu.make_async_copy(src, dst, rs(n)).start()
-
-    main_sends(0)
+        return qkv_st.at[:, pair, :, lanes], main.at[:, slot]
+
+    @pl.loop(1, 64)
+    def _(j):
+        i = (chip + j) % 64
+        src, dst = main_copy(i)
+        send(src, dst, ss(R_MAIN), rs(R_MAIN), zl, i * 2 + c).start()
+
+    src, dst = main_copy(chip)
+    pltpu.make_async_copy(src, dst, rs(R_MAIN)).start()
     w_slab = w_buf.at[c, pl.ds(y * 4, 4)]
     wait_for(w_slab, rs(R_WX))
     for j in range(1, 4):
         send(w_slab, w_slab, ss(R_W), rs(R_W), zl, seq_of((y + j) % 4, x, zh, c)).start()
-    main_sends(1)
     for i in range(4):
         down_all[i] = joined(down_v[i].astype(F32), down_sib[i].astype(F32))
     loads[5].wait()
     for i in range(4):
         up_cat[64 * i : 64 * (i + 1), :] = up_v[adapter[i]]
 
-    slab = kv.at[1, 0, :, pl.ds(x * 16, 16)]
+    slab = left.at[:, pl.ds(x * 16, 16)]
     wait_for(slab, rs(R_LEFT))
-    wait_for(q_buf.at[pl.ds(64, 16)], rs(R_LEFTQ))
+    wait_for(left_q, rs(R_LEFTQ))
 
     def ag_copy(j):
         return send(slab, slab, ss(R_AG), rs(R_AG), zl, seq_of(y, (x + j) % 4, zh, c))
 
     for j in range(1, 4):
         ag_copy(j).start()
-    wait_for(kv.at[1, 0, :, pl.ds(0, 48)], rs(R_AG))
-    ag_sib = send(kv.at[1, 0], kv.at[1, 1], ss(R_AGSIB), rs(R_AGSIB), zl, sib)
+    wait_for(left.at[:, pl.ds(0, 48)], rs(R_AG))
+    ag_sib = send(left, left_sib, ss(R_AGSIB), rs(R_AGSIB), zl, sib)
     ag_sib.start()
-    wait_for(kv.at[0, 0], rs(R_KV))
-    kv_sib = send(kv.at[0, 0], kv.at[0, 1], ss(R_KVSIB), rs(R_KVSIB), zl, sib)
+    wait_for(main, rs(R_MAIN))
+    kv_sib = send(main.at[pl.ds(1, 2)], main_sib, ss(R_KVSIB), rs(R_KVSIB), zl, sib)
     kv_sib.start()
-    wait_for(q_buf.at[pl.ds(0, 64)], rs(R_Q))
-    wait_for(kv.at[1, 1], rs(R_AGSIB))
-    wait_for(kv.at[0, 1], rs(R_KVSIB))
-
-    def attend(tile, which):
-        q = q_buf[pl.ds(tile * 16, 16)].reshape(256, 128)
+    wait_for(left_sib, rs(R_AGSIB))
+    wait_for(main_sib, rs(R_KVSIB))
+
+    def attend(q, keys, values, tile):
+        q = q.reshape(256, 128)
         scores = [
-            lax.dot_general(
-                q, kv[which, half, 0].reshape(1024, 128), (((1,), (1,)), ((), ())), preferred_element_type=F32
-            )
+            lax.dot_general(q, k.reshape(1024, 128), (((1,), (1,)), ((), ())), preferred_element_type=F32)
             * SCORE_SCALE
-            for half in range(2)
+            for k in keys
         ]
         top = jnp.maximum(
             jnp.max(scores[0], axis=1, keepdims=True), jnp.max(scores[1], axis=1, keepdims=True)
@@ -260,9 +251,12 @@
             weights = jnp.exp2(scores[half] - top)
             total = total + jnp.sum(weights, axis=1, keepdims=True)
             mixed = mixed + jnp.dot(
-                weights.astype(BF16), kv[which, half, 1].reshape(1024, 128), preferred_element_type=F32
+                weights.astype(BF16), values[half].reshape(1024, 128), preferred_element_type=F32
             )
         o_t[:, pl.ds(pl.multiple_of(tile * 256, 256), 256)] = jnp.transpose(mixed / total).astype(BF16)
+
+    def attend_main(tile):
+        attend(main[0, pl.ds(tile * 16, 16)], (main[1], main_sib[0]), (main[2], main_sib[1]), tile)
 
     unit0 = 12 * (x % 2) * (zh // 2) + 4 * (x % 2) * (1 - zh // 2) + 8 * (1 - x % 2) * (zh // 2)
     pair_all = 2 * zl + zh % 2
@@ -337,13 +331,13 @@
     def _(core2):
         @pl.loop(0, 2)
         def _(j):
-            attend(core2 * 2 + j, 0)
+            attend_main(core2 * 2 + j)
 
         @pl.loop(0, 8)
         def _(u):
             m1_start(core2 * 8 + u)
 
-    attend(4, 1)
+    attend(left_q[...], (left[0], left_sib[0]), (left[1], left_sib[1]), 4)
 
     @pl.loop(0, 4)
     def _(i):
@@ -465,18 +459,17 @@
 
     for copy in sib_copies:
         copy.wait_send()
-    wait_for(kv.at[1, 0, :, pl.ds(0, 15)], ss(R_LEFT))
-    wait_for(q_buf.at[pl.ds(0, 15)], ss(R_LEFTQ))
+    wait_for(left.at[:, pl.ds(0, 15)], ss(R_LEFT))
+    wait_for(left_q.at[pl.ds(0, 15)], ss(R_LEFTQ))
 
     @pl.when(x != y)
     def _():
         left_q_far.wait_send()
 
-    wait_for(kv.at[0, 0, :, pl.ds(0, 63)], ss(R_KV))
-    wait_for(q_buf.at[pl.ds(0, 63)], ss(R_Q))
+    wait_for(main.at[:, pl.ds(0, 63)], ss(R_MAIN))
     wait_for(w_buf.at[0, pl.ds(0, 3)], ss(R_WX))
     wait_for(w_buf.at[0, pl.ds(0, 12)], ss(R_W))
-    wait_for(kv.at[1, 0, :, pl.ds(0, 48)], ss(R_AG))
+    wait_for(left.at[:, pl.ds(0, 48)], ss(R_AG))
     ag_sib.wait_send()
     kv_sib.wait_send()
     w_fwd.wait_send()
@@ -519,8 +512,7 @@
         in_specs=[smem, smem] + [whole] * 6,
         out_specs=pl.BlockSpec(memory_space=pltpu.VMEM),
         scratch_shapes=[
-            vm((2, 16, 5120), BF16),
-            vm((2, 2, 16, 5120), BF16),
+            vm((3, 2, 16, 5120), BF16),
             vm((40, 5120), BF16),
             vm((4, 40, 640), BF16),
             vm((4, 80, 640), BF16),
@@ -530,8 +522,11 @@
             vm((4, 80, 64), BF16),
             vm((4, 64, 2560), BF16),
             vm((256, 2560), BF16),
-            vm((80, 16, 128), BF16),
-            vm((2, 2, 2, 64, 16, 128), BF16),
+            vm((3, 64, 16, 128), BF16),
+            vm((2, 64, 16, 128), BF16),
+            vm((16, 16, 128), BF16),
+            vm((2, 64, 16, 128), BF16),
+            vm((2, 64, 16, 128), BF16),
             vm((128, 1280), BF16),
             vm((4, 80, 512), BF16),
             vm((80, 512), BF16),
@@ -543,8 +538,8 @@
             vm((4, 16, 2560), BF16),
             vm((4, 16, 256), BF16),
             pltpu.SemaphoreType.DMA((6,)),
-            pltpu.SemaphoreType.DMA((17,)),
-            pltpu.SemaphoreType.DMA((17,)),
+            pltpu.SemaphoreType.DMA((16,)),
+            pltpu.SemaphoreType.DMA((16,)),
             pltpu.SemaphoreType.REGULAR,
         ],
         compiler_params=pltpu.CompilerParams(

time: 91.2 us -> 81.9 us (0.90)
  Pallas kernels: 88 us -> 78.7 us
    pallas_call x1, Pallas kernels: 88 us -> 78.7 us  [shards(): pl.pallas_call(body, out_shape=jax.ShapeDtypeStruct((16, 2560), F32), in_...]
where the time goes in v3:
time: 81.9 us; the launch traced here: 81.7 us
  Pallas kernels  78.7 us (96%)
  other arithmetic  2.35 us (3%)
    pallas_call x1, Pallas kernels, shards(): pl.pallas_call(body, out_shape=jax.ShapeDtypeStruct((16, 2560), F32), in_...  78.7 us

profile of v3, /device:TPU:1, one launch (start us, length us, event | category | flops | bytes accessed | tf_op | source)
XLA Modules:
  0.0 81.7 jit_solution(15693918462593311579)
XLA Ops:
  0.7 0.8 select_add_fusion
  1.4 78.7 %guided_attention.1 = f32[16,2560]{1,0:T(8,128)} custom-call(s32[4]{0:T(128)} %adapter.1, s32[4]{0:T(128)} %weight_eighths.1, bf16[2,16,5120]{2,1,0:T(8,128)(2,1)} %q_in.1, bf16[2,16,5120]{2,1,0:T(8,128)(2,1)} %k_in.1, bf16[2,16,5120]{2,1,0:T(8,128)(2,1)} %v_in.1, bf16[40,5120]{1,0:T(8,128)(2,1)} %w_in.1, bf16[4,40,64]{2,1,0:T(8,128)(2,1)} %down_in.1, ...), custom_call_target="tpu_custom_call" | custom-call | tf_op jit(solution)/shard_map/guided_attention/pallas_call | solution.py:509
  80.1 1.6 %multiply_convert_fusion = bf16[16,2560]{1,0:T(8,128)(2,1)} fusion(f32[16,2560]{1,0:T(8,128)} %guided_attention.1, f32[2560]{0:T(1024)S(1)} %select_add_fusion), kind=kLoop, calls=%fused_computation | loop fusion | flops 81920 | bytes 256000 | tf_op jit(solution)/shard_map/convert_element_type | solution.py:555

commit v4 on v3

--- a/solution.py
+++ b/solution.py
@@ -85,6 +85,7 @@
         R_LEFT,
         R_LEFTQ,
         R_MAIN,
+        R_Q,
         R_AG,
         R_AGSIB,
         R_KVSIB,
@@ -97,7 +98,8 @@
         R_LRF,
         R_SIBD,
         R_WX,
-    ) = range(16)
+        R_QS,
+    ) = range(18)
 
     def rs(i):
         return recv_sem.at[i]
@@ -197,43 +199,72 @@
         head = 5 * (2 * y2 + x2 // 2) + 3 * (x2 % 2) + z2 // 2
         lanes = pl.ds(pl.multiple_of(head * 128, 128), 128)
         pair = z2 % 2
-        return qkv_st.at[:, pair, :, lanes], main.at[:, slot]
-
-    @pl.loop(1, 64)
+        return (
+            (qkv_st.at[pl.ds(1, 2), pair, :, lanes], main.at[pl.ds(1, 2), slot]),
+            (qkv_st.at[0, pair, :, lanes], main.at[0, slot]),
+        )
+
+    def kv_start(j):
+        i = (chip + j) % 64
+        src, dst = main_copy(i)[0]
+        send(src, dst, ss(R_MAIN), rs(R_MAIN), zl, i * 2 + c).start()
+
+    @pl.loop(1, 24)
     def _(j):
-        i = (chip + j) % 64
-        src, dst = main_copy(i)
-        send(src, dst, ss(R_MAIN), rs(R_MAIN), zl, i * 2 + c).start()
-
-    src, dst = main_copy(chip)
+        kv_start(j)
+
+    slab = left.at[:, pl.ds(x * 16, 16)]
+    wait_for(slab, rs(R_LEFT))
+    for j in range(1, 4):
+        send(slab, slab, ss(R_AG), rs(R_AG), zl, seq_of(y, (x + j) % 4, zh, c)).start()
+
+    @pl.loop(24, 64)
+    def _(j):
+        kv_start(j)
+
+    src, dst = main_copy(chip)[0]
     pltpu.make_async_copy(src, dst, rs(R_MAIN)).start()
+
+    def flip(a, bit):
+        return (a + bit) % 2
+
+    def query_start(i):
+        x2 = 2 * flip(x // 2, i // 32) + flip(x % 2, (i // 4) % 2)
+        y2 = 2 * flip(y // 2, (i // 16) % 2) + flip(y % 2, (i // 8) % 2)
+        to = (y2 * 4 + x2) * 4 + (zh + i) % 4
+        src, dst = main_copy(to)[1]
+        send(src, dst, ss(R_Q), rs(R_QS + i // 16), zl, to * 2 + c).start()
+
+    src, dst = main_copy(chip)[1]
+    pltpu.make_async_copy(src, dst, rs(R_QS)).start()
+
     w_slab = w_buf.at[c, pl.ds(y * 4, 4)]
     wait_for(w_slab, rs(R_WX))
+    w_own_fwd = send(w_slab, w_slab, ss(R_WSIB), rs(R_WSIB), zl, sib)
+    w_own_fwd.start()
+
+    @pl.loop(1, 64)
+    def _(i):
+        query_start(i)
+
     for j in range(1, 4):
         send(w_slab, w_slab, ss(R_W), rs(R_W), zl, seq_of((y + j) % 4, x, zh, c)).start()
+
     for i in range(4):
         down_all[i] = joined(down_v[i].astype(F32), down_sib[i].astype(F32))
     loads[5].wait()
     for i in range(4):
         up_cat[64 * i : 64 * (i + 1), :] = up_v[adapter[i]]
 
-    slab = left.at[:, pl.ds(x * 16, 16)]
-    wait_for(slab, rs(R_LEFT))
     wait_for(left_q, rs(R_LEFTQ))
-
-    def ag_copy(j):
-        return send(slab, slab, ss(R_AG), rs(R_AG), zl, seq_of(y, (x + j) % 4, zh, c))
-
-    for j in range(1, 4):
-        ag_copy(j).start()
     wait_for(left.at[:, pl.ds(0, 48)], rs(R_AG))
     ag_sib = send(left, left_sib, ss(R_AGSIB), rs(R_AGSIB), zl, sib)
     ag_sib.start()
-    wait_for(main, rs(R_MAIN))
-    kv_sib = send(main.at[pl.ds(1, 2)], main_sib, ss(R_KVSIB), rs(R_KVSIB), zl, sib)
+    main_kv = main.at[pl.ds(1, 2)]
+    wait_for(main_kv, rs(R_MAIN))
+    kv_sib = send(main_kv, main_sib, ss(R_KVSIB), rs(R_KVSIB), zl, sib)
     kv_sib.start()
     wait_for(left_sib, rs(R_AGSIB))
-    wait_for(main_sib, rs(R_KVSIB))
 
     def attend(q, keys, values, tile):
         q = q.reshape(256, 128)
@@ -258,18 +289,40 @@
     def attend_main(tile):
         attend(main[0, pl.ds(tile * 16, 16)], (main[1], main_sib[0]), (main[2], main_sib[1]), tile)
 
-    unit0 = 12 * (x % 2) * (zh // 2) + 4 * (x % 2) * (1 - zh // 2) + 8 * (1 - x % 2) * (zh // 2)
+    places = (
+        ((0, 0), ((0, 80, 0, 0), (80, 48, 1, 0))),
+        ((0, 1), ((0, 32, 1, 48), (32, 80, 2, 0), (112, 16, 3, 0))),
+        ((1, 0), ((0, 16, 0, 64), (16, 80, 1, 0), (96, 32, 2, 0))),
+        ((1, 1), ((0, 48, 2, 32), (48, 80, 3, 0))),
+    )
     pair_all = 2 * zl + zh % 2
 
-    def m1_copy(i):
-        u = i % 8
-        core2 = i // 8
-        place = unit0 + u
-        z2 = place // 5
-        row = pl.multiple_of((place % 5) * 16, 16)
-        src = o_t.at[pl.ds(pl.multiple_of(u * 16, 16), 16), pl.ds(pl.multiple_of(core2 * 512, 512), 512)]
-        dst = m1.at[pair_all, pl.ds(row, 16)]
-        return src, dst, z2, core2
+    def m1_each(tile, action):
+        core2 = tile // 2
+        lanes = pl.ds(pl.multiple_of((tile % 2) * 256, 256), 256)
+        for (odd, which), pieces in places:
+
+            @pl.when(jnp.logical_and(x % 2 == odd, zh // 2 == which))
+            def _():
+                for first, count, z2, row in pieces:
+                    src = o_t.at[pl.ds(first, count), pl.ds(pl.multiple_of(tile * 256, 256), 256)]
+                    dst = m1.at[pair_all, pl.ds(row, count), lanes]
+                    mine = jnp.logical_and(jnp.logical_and(z2 == zh, c == zl), core2 == c)
+                    action(src, dst, mine, seq_of(y, x, z2, core2))
+
+    def m1_start(src, dst, mine, to):
+        @pl.when(mine)
+        def _():
+            pltpu.make_async_copy(src, dst, rs(R_M1)).start()
+
+        @pl.when(jnp.logical_not(mine))
+        def _():
+            send(src, dst, ss(R_M1), rs(R_M1), c, to).start()
+
+    def m1_wait_send(src, dst, mine, to):
+        @pl.when(jnp.logical_not(mine))
+        def _():
+            send(src, dst, ss(R_M1), rs(R_M1), c, to).wait_send()
 
     def m1_left_copy(i):
         odd = i % 2
@@ -282,26 +335,6 @@
         ]
         return src, dst, 2 * (zh // 2) + odd, 3 * (1 - odd), core2
 
-    def m1_start(i):
-        src, dst, z2, core2 = m1_copy(i)
-        mine = jnp.logical_and(jnp.logical_and(z2 == zh, c == zl), core2 == c)
-
-        @pl.when(mine)
-        def _():
-            pltpu.make_async_copy(src, dst, rs(R_M1)).start()
-
-        @pl.when(jnp.logical_not(mine))
-        def _():
-            send(src, dst, ss(R_M1), rs(R_M1), c, seq_of(y, x, z2, core2)).start()
-
-    def m1_wait_send(i):
-        src, dst, z2, core2 = m1_copy(i)
-        mine = jnp.logical_and(jnp.logical_and(z2 == zh, c == zl), core2 == c)
-
-        @pl.when(jnp.logical_not(mine))
-        def _():
-            send(src, dst, ss(R_M1), rs(R_M1), c, seq_of(y, x, z2, core2)).wait_send()
-
     def left_mine(x2, z2, core2):
         here = jnp.logical_and(x2 == x, z2 == zh)
         return jnp.logical_and(here, jnp.logical_and(c == zl, core2 == c))
@@ -326,26 +359,21 @@
             send(src, dst, ss(R_M1), rs(R_M1), c, seq_of(y, x2, z2, core2)).wait_send()
 
     pl.semaphore_wait(token, 1)
-
-    @pl.loop(0, 2)
-    def _(core2):
-        @pl.loop(0, 2)
-        def _(j):
-            attend_main(core2 * 2 + j)
-
-        @pl.loop(0, 8)
-        def _(u):
-            m1_start(core2 * 8 + u)
-
     attend(left_q[...], (left[0], left_sib[0]), (left[1], left_sib[1]), 4)
 
     @pl.loop(0, 4)
     def _(i):
         m1_left_start(i)
 
-    wait_for(w_buf.at[0, pl.ds(0, 12)], rs(R_W))
-    w_fwd = send(w_buf.at[c], w_buf.at[c], ss(R_WSIB), rs(R_WSIB), zl, sib)
-    w_fwd.start()
+    wait_for(main_sib, rs(R_KVSIB))
+
+    @pl.loop(0, 4)
+    def _(t):
+        tile = 2 * flip(x // 2, t // 2) + flip(y // 2, t % 2)
+        wait_for(main.at[0, pl.ds(0, 16)], rs(R_QS + t))
+        attend_main(tile)
+
+        m1_each(tile, m1_start)
 
     wait_for(m1, rs(R_M1))
     guide = [weight_eighths[i].astype(F32) * GUIDE_UNIT for i in range(4)]
@@ -366,6 +394,15 @@
 
     src, dst = m2_copy(col)
     pltpu.make_async_copy(src, dst, rs(R_M2)).start()
+
+    wait_for(w_buf.at[0, pl.ds(0, 12)], rs(R_W))
+
+    def w_fwd(j):
+        rows = w_buf.at[c, pl.ds((y + j) % 4 * 4, 4)]
+        return send(rows, rows, ss(R_WSIB), rs(R_WSIB), zl, sib)
+
+    for j in range(1, 4):
+        w_fwd(j).start()
 
     ranks = jnp.concatenate(
         [
@@ -395,30 +432,36 @@
     wait_for(w_buf.at[0], rs(R_WSIB))
     wait_for(m2, rs(R_M2))
     rows = jnp.transpose(m2[...].reshape(1280, 128).astype(F32)).astype(BF16)
-    for half in range(2):
+    def project(half):
         p_out[:, 640 * half : 640 * (half + 1)] = jnp.dot(
             rows, w_buf[half].reshape(1280, 640), preferred_element_type=F32
         ).astype(BF16)
 
-    def p_copy(i):
+    def p_copy(i, half):
         x2 = 2 * c + i // 4
         z2 = i % 4
-        src = p_out.at[pl.ds(pl.multiple_of(i * 16, 16), 16)]
-        dst = p_got.at[zh, :, pl.ds(pl.multiple_of((x % 2) * 1280, 1280), 1280)]
+        src = p_out.at[pl.ds(pl.multiple_of(i * 16, 16), 16), pl.ds(640 * half, 640)]
+        dst = p_got.at[zh, :, pl.ds(pl.multiple_of((x % 2) * 1280 + 640 * half, 128), 640)]
         here = jnp.logical_and(jnp.logical_and(x2 == x, z2 == zh), x // 2 == zl)
         return src, dst, seq_of(y, x2, z2, zl), jnp.logical_and(here, c == zl)
 
-    @pl.loop(0, 8)
-    def _(i):
-        src, dst, to, mine = p_copy(i)
-
-        @pl.when(mine)
-        def _():
-            pltpu.make_async_copy(src, dst, rs(R_P)).start()
-
-        @pl.when(jnp.logical_not(mine))
-        def _():
-            send(src, dst, ss(R_P), rs(R_P), x // 2, to).start()
+    def p_start(half):
+        @pl.loop(0, 8)
+        def _(i):
+            src, dst, to, mine = p_copy(i, half)
+
+            @pl.when(mine)
+            def _():
+                pltpu.make_async_copy(src, dst, rs(R_P)).start()
+
+            @pl.when(jnp.logical_not(mine))
+            def _():
+                send(src, dst, ss(R_P), rs(R_P), x // 2, to).start()
+
+    project(0)
+    p_start(0)
+    project(1)
+    p_start(1)
 
     wait_for(lr_got, rs(R_LR))
     low = lr_got[0].astype(F32)
@@ -466,17 +509,18 @@
     def _():
         left_q_far.wait_send()
 
-    wait_for(main.at[:, pl.ds(0, 63)], ss(R_MAIN))
+    wait_for(main.at[pl.ds(1, 2), pl.ds(0, 63)], ss(R_MAIN))
+    wait_for(main.at[0, pl.ds(0, 63)], ss(R_Q))
     wait_for(w_buf.at[0, pl.ds(0, 3)], ss(R_WX))
     wait_for(w_buf.at[0, pl.ds(0, 12)], ss(R_W))
     wait_for(left.at[:, pl.ds(0, 48)], ss(R_AG))
     ag_sib.wait_send()
     kv_sib.wait_send()
-    w_fwd.wait_send()
-
-    @pl.loop(0, 16)
-    def _(i):
-        m1_wait_send(i)
+    wait_for(w_buf.at[0], ss(R_WSIB))
+
+    @pl.loop(0, 4)
+    def _(tile):
+        m1_each(tile, m1_wait_send)
 
     @pl.loop(0, 4)
     def _(i):
@@ -485,13 +529,15 @@
     wait_for(m2.at[pl.ds(0, 15)], ss(R_M2))
     wait_for(lr_got.at[pl.ds(0, 15)], ss(R_LR))
 
-    @pl.loop(0, 8)
-    def _(i):
-        src, dst, to, mine = p_copy(i)
-
-        @pl.when(jnp.logical_not(mine))
-        def _():
-            send(src, dst, ss(R_P), rs(R_P), x // 2, to).wait_send()
+    for half in range(2):
+
+        @pl.loop(0, 8)
+        def _(i):
+            src, dst, to, mine = p_copy(i, half)
+
+            @pl.when(jnp.logical_not(mine))
+            def _():
+                send(src, dst, ss(R_P), rs(R_P), x // 2, to).wait_send()
 
     @pl.loop(0, 4)
     def _(i):
@@ -538,8 +584,8 @@
             vm((4, 16, 2560), BF16),
             vm((4, 16, 256), BF16),
             pltpu.SemaphoreType.DMA((6,)),
-            pltpu.SemaphoreType.DMA((16,)),
-            pltpu.SemaphoreType.DMA((16,)),
+            pltpu.SemaphoreType.DMA((17,)),
+            pltpu.SemaphoreType.DMA((21,)),
             pltpu.SemaphoreType.REGULAR,
         ],
         compiler_params=pltpu.CompilerParams(

time: 81.9 us -> 78.1 us (0.954)
  Pallas kernels: 78.7 us -> 74.9 us
    pallas_call x1, Pallas kernels: 78.7 us -> 74.9 us  [shards(): pl.pallas_call(body, out_shape=jax.ShapeDtypeStruct((16, 2560), F32), in_...]
where the time goes in v4:
time: 78.1 us; the launch traced here: 77.9 us
  Pallas kernels  74.9 us (96%)
  other arithmetic  2.35 us (3%)
    pallas_call x1, Pallas kernels, shards(): pl.pallas_call(body, out_shape=jax.ShapeDtypeStruct((16, 2560), F32), in_...  74.9 us
    convert_element_type x1, other arithmetic, shards(): return (mixture * gate_row[None, :]).astype(BF16)  1.57 us

profile of v4, /device:TPU:1, one launch (start us, length us, event | category | flops | bytes accessed | tf_op | source)
XLA Modules:
  0.0 77.9 jit_solution(3112662579780137947)
XLA Ops:
  0.7 0.8 %select_add_fusion = f32[2560]{0:T(1024)S(1)} fusion(f32[2560]{0:T(1024)} %param.18, f32[]{:T(128)} %bitcast, s32[]{:T(128)S(6)} %mul.23), kind=kLoop, calls=%fused_computation.6 | loop fusion | flops 33280 | bytes 20488 | tf_op jit(solution)/shard_map/add | solution.py:600
  1.4 74.9 %guided_attention.1 = f32[16,2560]{1,0:T(8,128)} custom-call(s32[4]{0:T(128)} %adapter.1, s32[4]{0:T(128)} %weight_eighths.1, bf16[2,16,5120]{2,1,0:T(8,128)(2,1)} %q_in.1, bf16[2,16,5120]{2,1,0:T(8,128)(2,1)} %k_in.1, bf16[2,16,5120]{2,1,0:T(8,128)(2,1)} %v_in.1, bf16[40,5120]{1,0:T(8,128)(2,1)} %w_in.1, bf16[4,40,64]{2,1,0:T(8,128)(2,1)} %down_in.1, ...), custom_call_target="tpu_custom_call" | custom-call | tf_op jit(solution)/shard_map/guided_attention/pallas_call | solution.py:555
  76.4 1.6 %multiply_convert_fusion = bf16[16,2560]{1,0:T(8,128)(2,1)} fusion(f32[16,2560]{1,0:T(8,128)} %guided_attention.1, f32[2560]{0:T(1024)S(1)} %select_add_fusion), kind=kLoop, calls=%fused_computation | loop fusion | flops 81920 | bytes 256000 | tf_op jit(solution)/shard_map/convert_element_type | solution.py:601

commit v5 on v4

--- a/solution.py
+++ b/solution.py
@@ -132,7 +132,7 @@
 
     sib_copies = [
         send(
-            w_v.at[:, pl.ds(pl.multiple_of(1280 * i + 640 * (1 - c), 128), 640)],
+            w_v.at[:, pl.ds(pl.multiple_of(640 * i + 2560 * (1 - c), 128), 640)],
             w_sib.at[i],
             ss(R_SIBW),
             rs(R_SIBW),
@@ -155,7 +155,7 @@
         return jnp.concatenate([first, second], axis=0).astype(BF16)
 
     for i in range(4):
-        own = w_v[:, pl.ds(pl.multiple_of(1280 * i + 640 * c, 128), 640)].astype(F32)
+        own = w_v[:, pl.ds(pl.multiple_of(640 * i + 2560 * c, 128), 640)].astype(F32)
         w_st[i] = joined(own, w_sib[i].astype(F32))
     for j in range(1, 4):
         i = (x + j) % 4
@@ -441,8 +441,8 @@
         x2 = 2 * c + i // 4
         z2 = i % 4
         src = p_out.at[pl.ds(pl.multiple_of(i * 16, 16), 16), pl.ds(640 * half, 640)]
-        dst = p_got.at[zh, :, pl.ds(pl.multiple_of((x % 2) * 1280 + 640 * half, 128), 640)]
-        here = jnp.logical_and(jnp.logical_and(x2 == x, z2 == zh), x // 2 == zl)
+        dst = p_got.at[zh, :, pl.ds(pl.multiple_of(640 * x, 128), 640)]
+        here = jnp.logical_and(jnp.logical_and(x2 == x, z2 == zh), zl == half)
         return src, dst, seq_of(y, x2, z2, zl), jnp.logical_and(here, c == zl)
 
     def p_start(half):
@@ -456,7 +456,7 @@
 
             @pl.when(jnp.logical_not(mine))
             def _():
-                send(src, dst, ss(R_P), rs(R_P), x // 2, to).start()
+                send(src, dst, ss(R_P), rs(R_P), half, to).start()
 
     project(0)
     p_start(0)
@@ -537,7 +537,7 @@
 
             @pl.when(jnp.logical_not(mine))
             def _():
-                send(src, dst, ss(R_P), rs(R_P), x // 2, to).wait_send()
+                send(src, dst, ss(R_P), rs(R_P), half, to).wait_send()
 
     @pl.loop(0, 4)
     def _(i):

time: 78.1 us -> 75.4 us (0.965)
  Pallas kernels: 74.9 us -> 71.5 us
    pallas_call x1, Pallas kernels: 74.9 us -> 71.5 us  [shards(): pl.pallas_call(body, out_shape=jax.ShapeDtypeStruct((16, 2560), F32), in_...]
where the time goes in v5:
time: 75.4 us; the launch traced here: 74.5 us
  Pallas kernels  71.5 us (95%)
  other arithmetic  2.35 us (3%)
    pallas_call x1, Pallas kernels, shards(): pl.pallas_call(body, out_shape=jax.ShapeDtypeStruct((16, 2560), F32), in_...  71.5 us
    convert_element_type x1, other arithmetic, shards(): return (mixture * gate_row[None, :]).astype(BF16)  1.57 us

profile of v5, /device:TPU:1, one launch (start us, length us, event | category | flops | bytes accessed | tf_op | source)
XLA Modules:
  0.0 74.5 jit_solution(15315238413564270955)
XLA Ops:
  0.7 0.8 %select_add_fusion = f32[2560]{0:T(1024)S(1)} fusion(f32[2560]{0:T(1024)} %param.18, f32[]{:T(128)} %bitcast, s32[]{:T(128)S(6)} %mul.23), kind=kLoop, calls=%fused_computation.6 | loop fusion | flops 33280 | bytes 20488 | tf_op jit(solution)/shard_map/add | solution.py:600
  1.4 71.5 %guided_attention.1 = f32[16,2560]{1,0:T(8,128)} custom-call(s32[4]{0:T(128)} %adapter.1, s32[4]{0:T(128)} %weight_eighths.1, bf16[2,16,5120]{2,1,0:T(8,128)(2,1)} %q_in.1, bf16[2,16,5120]{2,1,0:T(8,128)(2,1)} %k_in.1, bf16[2,16,5120]{2,1,0:T(8,128)(2,1)} %v_in.1, bf16[40,5120]{1,0:T(8,128)(2,1)} %w_in.1, bf16[4,40,64]{2,1,0:T(8,128)(2,1)} %down_in.1, ...), custom_call_target="tpu_custom_call" | custom-call | tf_op jit(solution)/shard_map/guided_attention/pallas_call | solution.py:555
  73.0 1.6 %multiply_convert_fusion = bf16[16,2560]{1,0:T(8,128)(2,1)} fusion(f32[16,2560]{1,0:T(8,128)} %guided_attention.1, f32[2560]{0:T(1024)S(1)} %select_add_fusion), kind=kLoop, calls=%fused_computation | loop fusion | flops 81920 | bytes 256000 | tf_op jit(solution)/shard_map/convert_element_type | solution.py:601

commit v6 on v5

--- a/solution.py
+++ b/solution.py
@@ -32,6 +32,8 @@
 def body(
     adapter,
     weight_eighths,
+    timestep,
+    gate_offset,
     q_in,
     k_in,
     v_in,
@@ -64,6 +66,7 @@
     p_out,
     p_got,
     lr_fin,
+    gate,
     in_sem,
     send_sem,
     recv_sem,
@@ -114,13 +117,15 @@
         pltpu.make_async_copy(v_in, qkv_st.at[2], in_sem.at[3]),
         pltpu.make_async_copy(q_in, qkv_st.at[0], in_sem.at[4]),
         pltpu.make_async_copy(up_in.at[:, :, pl.ds(pl.multiple_of(zl * 2560, 2560), 2560)], up_v, in_sem.at[5]),
+        pltpu.make_async_copy(gate_offset, gate.at[0], in_sem.at[6]),
     ]
     for load in loads:
         load.start()
 
+
     barrier = pltpu.get_barrier_semaphore()
 
-    @pl.loop(1, 64)
+    @pl.loop(1, 64, unroll=9)
     def _(i):
         pl.semaphore_signal(barrier, 1, device_id=(zl, ((chip + i) % 64) * 2 + c), device_id_type=MESH)
 
@@ -209,7 +214,7 @@
         src, dst = main_copy(i)[0]
         send(src, dst, ss(R_MAIN), rs(R_MAIN), zl, i * 2 + c).start()
 
-    @pl.loop(1, 24)
+    @pl.loop(1, 50)
     def _(j):
         kv_start(j)
 
@@ -218,7 +223,7 @@
     for j in range(1, 4):
         send(slab, slab, ss(R_AG), rs(R_AG), zl, seq_of(y, (x + j) % 4, zh, c)).start()
 
-    @pl.loop(24, 64)
+    @pl.loop(50, 64)
     def _(j):
         kv_start(j)
 
@@ -253,6 +258,10 @@
     for i in range(4):
         down_all[i] = joined(down_v[i].astype(F32), down_sib[i].astype(F32))
     loads[5].wait()
+    place = lax.broadcasted_iota(jnp.int32, (1, 2560), 1).astype(F32)
+    angles = timestep[0].astype(F32) * jnp.exp(place * (-math.log(10000.0) / 2560))
+    loads[6].wait()
+    gate[...] = gate[...] + jnp.where(zl == 0, jnp.cos(angles), jnp.sin(angles))
     for i in range(4):
         up_cat[64 * i : 64 * (i + 1), :] = up_v[adapter[i]]
 
@@ -498,7 +507,7 @@
     wait_for(p_got, rs(R_P))
     for i in range(4):
         adapted = adapted + p_got[i].astype(F32)
-    out[...] = adapted
+    out[...] = (adapted * gate[...]).astype(BF16)
 
     for copy in sib_copies:
         copy.wait_send()
@@ -552,10 +561,10 @@
     whole = pl.BlockSpec(memory_space=pl.ANY)
     smem = pl.BlockSpec(memory_space=pltpu.SMEM)
     vm = pltpu.VMEM
-    mixture = pl.pallas_call(
+    return pl.pallas_call(
         body,
-        out_shape=jax.ShapeDtypeStruct((16, 2560), F32),
-        in_specs=[smem, smem] + [whole] * 6,
+        out_shape=jax.ShapeDtypeStruct((16, 2560), BF16),
+        in_specs=[smem] * 3 + [whole] * 7,
         out_specs=pl.BlockSpec(memory_space=pltpu.VMEM),
         scratch_shapes=[
             vm((3, 2, 16, 5120), BF16),
@@ -583,7 +592,8 @@
             vm((128, 1280), BF16),
             vm((4, 16, 2560), BF16),
             vm((4, 16, 256), BF16),
-            pltpu.SemaphoreType.DMA((6,)),
+            vm((1, 2560), F32),
+            pltpu.SemaphoreType.DMA((7,)),
             pltpu.SemaphoreType.DMA((17,)),
             pltpu.SemaphoreType.DMA((21,)),
             pltpu.SemaphoreType.REGULAR,
@@ -592,13 +602,7 @@
             collective_id=0, has_side_effects=True, vmem_limit_bytes=62 * 2**20
         ),
         name="guided_attention",
-    )(adapter, weight_eighths, q, k, v, w, down, up)
-
-    columns = lax.axis_index("branch") * 2560 + jnp.arange(2560, dtype=jnp.int32)
-    frequency = jnp.exp((columns % 2560).astype(F32) * (-math.log(10000.0) / 2560))
-    angles = timestep.astype(F32)[0] * frequency
-    gate_row = gate_offset + jnp.where(columns < 2560, jnp.cos(angles), jnp.sin(angles))
-    return (mixture * gate_row[None, :]).astype(BF16)
+    )(adapter, weight_eighths, timestep, gate_offset, q, k, v, w, down, up)
 
 
 def solution(mesh):

time: 75.4 us -> 72.8 us (0.966)
  other arithmetic: 2.35 us -> 0 us
  local copies, waits for them, and re-layouts: 0 us -> 1.53 us
  Pallas kernels: 71.5 us -> 70.4 us
    convert_element_type x1 -> x0, other arithmetic: 1.57 us -> none  [shards(): return (mixture * gate_row[None, :]).astype(BF16)]
    unnamed x0 -> x1, local copies, waits for them, and re-layouts: none -> 1.53 us
    pallas_call x1, Pallas kernels: 71.5 us -> 70.4 us  [shards(): pl.pallas_call(body, out_shape=jax.ShapeDtypeStruct((16, 2560), BF16), in...]
    add x1 -> x0, other arithmetic: 0.78 us -> none  [shards(): gate_offset + jnp.where(columns < 2560, jnp.cos(angles), jnp.sin(angles))]
where the time goes in v6:
time: 72.8 us; the launch traced here: 72.6 us
  Pallas kernels  70.4 us (97%)
  local copies, waits for them, and re-layouts  1.53 us (2%)
    pallas_call x1, Pallas kernels, shards(): pl.pallas_call(body, out_shape=jax.ShapeDtypeStruct((16, 2560), BF16), in...  70.4 us
    unnamed x1, local copies, waits for them, and re-layouts  1.53 us

profile of v6, /device:TPU:1, one launch (start us, length us, event | category | flops | bytes accessed | tf_op | source)
XLA Modules:
  0.0 72.6 jit_solution(968613092922513851)
XLA Ops:
  0.7 70.4 %guided_attention.1 = bf16[16,2560]{1,0:T(8,128)(2,1)} custom-call(s32[4]{0:T(128)} %adapter.1, s32[4]{0:T(128)} %weight_eighths.1, s32[1]{0:T(128)S(6)} %copy.12.timestep, f32[2560]{0:T(1024)} %gate_offset.1, bf16[2,16,5120]{2,1,0:T(8,128)(2,1)} %q_in.1, bf16[2,16,5120]{2,1,0:T(8,128)(2,1)} %k_in.1, bf16[2,16,5120]{2,1,0:T(8,128)(2,1)} %v_in.1, ...), custom_call_target="tpu_custom_call" | custom-call | tf_op jit(solution)/shard_map/guided_attention/pallas_call | solution.py:564
  71.1 1.5 %copy.13 = bf16[16,2560]{1,0:T(8,128)(2,1)} copy(bf16[16,2560]{1,0:T(8,128)(2,1)} %guided_attention.1) | data formatting | bytes 163840

commit v7 on v6

--- a/solution.py
+++ b/solution.py
@@ -150,23 +150,6 @@
     for copy in sib_copies:
         copy.start()
 
-    wait_for(w_sib, rs(R_SIBW))
-    wait_for(down_sib, rs(R_SIBD))
-    pl.semaphore_signal(token, 1, device_id=(1 - zl, s), device_id_type=MESH)
-
-    def joined(own, other):
-        first = jnp.where(c == 0, own, other)
-        second = jnp.where(c == 0, other, own)
-        return jnp.concatenate([first, second], axis=0).astype(BF16)
-
-    for i in range(4):
-        own = w_v[:, pl.ds(pl.multiple_of(640 * i + 2560 * c, 128), 640)].astype(F32)
-        w_st[i] = joined(own, w_sib[i].astype(F32))
-    for j in range(1, 4):
-        i = (x + j) % 4
-        send(w_st.at[i], w_buf.at[c, col], ss(R_WX), rs(R_WX), zl, seq_of(y, i, zh, c)).start()
-    pltpu.make_async_copy(w_st.at[x], w_buf.at[c, col], rs(R_WX)).start()
-
     def left_copy(i):
         y2 = i // 4
         z2 = i % 4
@@ -214,14 +197,30 @@
         src, dst = main_copy(i)[0]
         send(src, dst, ss(R_MAIN), rs(R_MAIN), zl, i * 2 + c).start()
 
-    @pl.loop(1, 50)
+    @pl.loop(1, 9)
     def _(j):
         kv_start(j)
 
-    slab = left.at[:, pl.ds(x * 16, 16)]
-    wait_for(slab, rs(R_LEFT))
+    wait_for(w_sib, rs(R_SIBW))
+    wait_for(down_sib, rs(R_SIBD))
+    pl.semaphore_signal(token, 1, device_id=(1 - zl, s), device_id_type=MESH)
+
+    def joined(own, other):
+        first = jnp.where(c == 0, own, other)
+        second = jnp.where(c == 0, other, own)
+        return jnp.concatenate([first, second], axis=0).astype(BF16)
+
+    for i in range(4):
+        own = w_v[:, pl.ds(pl.multiple_of(640 * i + 2560 * c, 128), 640)].astype(F32)
+        w_st[i] = joined(own, w_sib[i].astype(F32))
     for j in range(1, 4):
-        send(slab, slab, ss(R_AG), rs(R_AG), zl, seq_of(y, (x + j) % 4, zh, c)).start()
+        i = (x + j) % 4
+        send(w_st.at[i], w_buf.at[c, col], ss(R_WX), rs(R_WX), zl, seq_of(y, i, zh, c)).start()
+    pltpu.make_async_copy(w_st.at[x], w_buf.at[c, col], rs(R_WX)).start()
+
+    @pl.loop(9, 50)
+    def _(j):
+        kv_start(j)
 
     @pl.loop(50, 64)
     def _(j):
@@ -248,7 +247,16 @@
     w_own_fwd = send(w_slab, w_slab, ss(R_WSIB), rs(R_WSIB), zl, sib)
     w_own_fwd.start()
 
-    @pl.loop(1, 64)
+    @pl.loop(1, 16)
+    def _(i):
+        query_start(i)
+
+    slab = left.at[:, pl.ds(x * 16, 16)]
+    wait_for(slab, rs(R_LEFT))
+    for j in range(1, 4):
+        send(slab, slab, ss(R_AG), rs(R_AG), zl, seq_of(y, (x + j) % 4, zh, c)).start()
+
+    @pl.loop(16, 64)
     def _(i):
         query_start(i)
 

time: 72.8 us -> 71.5 us (0.982); the launches traced: 72.6 us -> 70.5 us
  Pallas kernels: 70.4 us -> 68.3 us
    pallas_call x1, Pallas kernels: 70.4 us -> 68.3 us  [shards(): pl.pallas_call(body, out_shape=jax.ShapeDtypeStruct((16, 2560), BF16), in...]
where the time goes in v7:
time: 71.5 us; the launch traced here: 70.5 us
  Pallas kernels  68.3 us (96%)
  local copies, waits for them, and re-layouts  1.53 us (2%)
    pallas_call x1, Pallas kernels, shards(): pl.pallas_call(body, out_shape=jax.ShapeDtypeStruct((16, 2560), BF16), in...  68.3 us
    unnamed x1, local copies, waits for them, and re-layouts  1.53 us

profile of v7, /device:TPU:1, one launch (start us, length us, event | category | flops | bytes accessed | tf_op | source)
XLA Modules:
  0.0 70.5 jit_solution(10748234529734180945)
XLA Ops:
  0.7 68.3 %guided_attention.1 = bf16[16,2560]{1,0:T(8,128)(2,1)} custom-call(s32[4]{0:T(128)} %adapter.1, s32[4]{0:T(128)} %weight_eighths.1, s32[1]{0:T(128)S(6)} %copy.12.timestep, f32[2560]{0:T(1024)} %gate_offset.1, bf16[2,16,5120]{2,1,0:T(8,128)(2,1)} %q_in.1, bf16[2,16,5120]{2,1,0:T(8,128)(2,1)} %k_in.1, bf16[2,16,5120]{2,1,0:T(8,128)(2,1)} %v_in.1, ...), custom_call_target="tpu_custom_call" | custom-call | tf_op jit(solution)/shard_map/guided_attention/pallas_call | solution.py:572
  69.0 1.5 %copy.13 = bf16[16,2560]{1,0:T(8,128)(2,1)} copy(bf16[16,2560]{1,0:T(8,128)(2,1)} %guided_attention.1) | data formatting | bytes 163840

commit v8 on v7

--- a/solution.py
+++ b/solution.py
@@ -242,23 +242,23 @@
     src, dst = main_copy(chip)[1]
     pltpu.make_async_copy(src, dst, rs(R_QS)).start()
 
+    @pl.loop(1, 16)
+    def _(i):
+        query_start(i)
+
+    slab = left.at[:, pl.ds(x * 16, 16)]
+    wait_for(slab, rs(R_LEFT))
+    for j in range(1, 4):
+        send(slab, slab, ss(R_AG), rs(R_AG), zl, seq_of(y, (x + j) % 4, zh, c)).start()
+
+    @pl.loop(16, 64)
+    def _(i):
+        query_start(i)
+
     w_slab = w_buf.at[c, pl.ds(y * 4, 4)]
     wait_for(w_slab, rs(R_WX))
     w_own_fwd = send(w_slab, w_slab, ss(R_WSIB), rs(R_WSIB), zl, sib)
     w_own_fwd.start()
-
-    @pl.loop(1, 16)
-    def _(i):
-        query_start(i)
-
-    slab = left.at[:, pl.ds(x * 16, 16)]
-    wait_for(slab, rs(R_LEFT))
-    for j in range(1, 4):
-        send(slab, slab, ss(R_AG), rs(R_AG), zl, seq_of(y, (x + j) % 4, zh, c)).start()
-
-    @pl.loop(16, 64)
-    def _(i):
-        query_start(i)
 
     for j in range(1, 4):
         send(w_slab, w_slab, ss(R_W), rs(R_W), zl, seq_of((y + j) % 4, x, zh, c)).start()

time: 71.5 us -> 71.7 us (level)
  the two profiles are of different devices: /device:TPU:1 before, /device:TPU:2 now
where the time goes in v8:
time: 71.7 us; the launch traced here: 71.6 us
  Pallas kernels  69.4 us (97%)
  local copies, waits for them, and re-layouts  1.53 us (2%)
    pallas_call x1, Pallas kernels, shards(): pl.pallas_call(body, out_shape=jax.ShapeDtypeStruct((16, 2560), BF16), in...  69.4 us
    unnamed x1, local copies, waits for them, and re-layouts  1.53 us

profile of v8, /device:TPU:2, one launch (start us, length us, event | category | flops | bytes accessed | tf_op | source)
XLA Modules:
  0.0 71.6 jit_solution(17841664599879548623)
XLA Ops:
  0.7 69.4 %guided_attention.1 = bf16[16,2560]{1,0:T(8,128)(2,1)} custom-call(s32[4]{0:T(128)} %adapter.1, s32[4]{0:T(128)} %weight_eighths.1, s32[1]{0:T(128)S(6)} %copy.12.timestep, f32[2560]{0:T(1024)} %gate_offset.1, bf16[2,16,5120]{2,1,0:T(8,128)(2,1)} %q_in.1, bf16[2,16,5120]{2,1,0:T(8,128)(2,1)} %k_in.1, bf16[2,16,5120]{2,1,0:T(8,128)(2,1)} %v_in.1, ...), custom_call_target="tpu_custom_call" | custom-call | tf_op jit(solution)/shard_map/guided_attention/pallas_call | solution.py:572
  70.0 1.5 %copy.13 = bf16[16,2560]{1,0:T(8,128)(2,1)} copy(bf16[16,2560]{1,0:T(8,128)(2,1)} %guided_attention.1) | data formatting | bytes 163840
